TPU v7x, 32 devices: a whole 2x2x4 slice. The times are simulated.
32 devices in a mesh: groups: 2 (over x), shard: 16 (over z, y, core).
Axes of the slice: x: 2, y: 2, z: 4, core: 2. Of those that a mesh axis runs over, the one named last changes fastest.
Arguments:
- tokens: bfloat16 [8192, 8192], P(('groups', 'shard')), parts along dimension 0, may hold values from -6 to 6
- cotangent: bfloat16 [8192, 1024], P(('groups', 'shard')), parts along dimension 0, may hold values from -6 to 6
- response_loss_mask: int32 [8192], P(('groups', 'shard')), parts along dimension 0, may hold values 0 or 1
- adapter_down_weight: bfloat16 [64, 8192], P(None, 'shard'), may hold values from -0.0625 to 0.0625
- projection: bfloat16 [65536, 4096], P('shard'), may hold values from -0.0234375 to 0.0234375
- targets: float32 [256, 4096], P(('groups', 'shard')), parts along dimension 0, may hold values from -6 to 6
Outputs:
- scores: float32 [32, 128], P('groups', 'shard'), parts along dimension 0
There are 2 independent parts, one for each index of `groups`. A program takes and returns all parts, laid end to end along the dimension named above; an argument that names none is the same for every part. Nothing has to cross between parts.
All inputs are finite; a program needn't handle non-finite values. No bound on the sum of `response_loss_mask` on one device may be relied on, other than what follows from the above.
Results may differ from a plain program's by a relative error of at most 0.004.
Values may be sent and summed in bfloat16 or wider, within the bound.
No kernel may reach another device: no remote copies, remote signals or barrier semaphores. Data moves between devices by JAX's collectives and lax.ppermute only.
A program may use at most 128 MiB of HBM per device.

v0:
```python
import functools

import jax
import jax.numpy as jnp
from jax import lax
from jax.experimental import pallas as pl
from jax.experimental.pallas import tpu as pltpu
from jax.sharding import PartitionSpec as P

PDIM = 4096
LENGTH = 256
LANES = 256
NEAR = 4
MIB = 1 << 20
HIDE = 30 * 10**9
NT = (((1,), (1,)), ((), ()))
VMEM = pl.BlockSpec(memory_space=pltpu.VMEM)
SMEM = pl.BlockSpec(memory_space=pltpu.SMEM)
ANY = pl.BlockSpec(memory_space=pl.ANY)


def swap(value, bit, n):
    return lax.ppermute(value, "shard", [(s, s ^ bit) for s in range(n)])


def span(bits):
    sums = [0]
    for bit in bits:
        sums += [k + bit for k in sums]
    return sums


def in_hbm(value):
    return pltpu.with_memory_space_constraint(value, pltpu.HBM)


def in_vmem(value):
    return pltpu.with_memory_space_constraint(value, pltpu.VMEM)


def load_kernel(count, starts, *refs):
    sources, outs, sems = refs[:count], refs[-1 - count : -1], refs[-1]
    copies = []
    for source, start, out in zip(sources, starts, outs):
        rows = out.shape[0]
        step = min(rows, LANES // 2)
        for i in range(0, rows, step):
            part = source.at[pl.ds(start + i, step)]
            copies.append(pltpu.make_async_copy(part, out.at[pl.ds(i, step)], sems.at[len(copies)]))
    for copy in copies:
        copy.start()
    for copy in copies:
        copy.wait()


def load(name, parts, after):
    size = sum(rows * array.size // array.shape[0] * array.dtype.itemsize for array, _, rows in parts)
    pieces = sum(max(rows // (LANES // 2), 1) for _, _, rows in parts)
    return pl.pallas_call(
        functools.partial(load_kernel, len(parts), [start for _, start, _ in parts]),
        out_shape=[pltpu.VMEM((rows,) + array.shape[1:], array.dtype) for array, _, rows in parts],
        in_specs=[ANY] * (len(parts) + len(after)),
        out_specs=[VMEM] * len(parts),
        scratch_shapes=[pltpu.SemaphoreType.DMA((pieces,))],
        compiler_params=pltpu.CompilerParams(vmem_limit_bytes=MIB),
        cost_estimate=pl.CostEstimate(flops=0, bytes_accessed=2 * size, transcendentals=0),
        name=name,
    )(*[in_hbm(array) for array, _, _ in parts], *after)


def hold(name, value, after, flops=0):
    return pl.pallas_call(
        lambda *refs: None,
        out_shape=jax.ShapeDtypeStruct(value.shape, value.dtype),
        in_specs=[ANY] * (1 + len(after)),
        out_specs=ANY,
        input_output_aliases={0: 0},
        compiler_params=pltpu.CompilerParams(vmem_limit_bytes=MIB),
        cost_estimate=pl.CostEstimate(flops=flops, bytes_accessed=2000000, transcendentals=0),
        name=name,
    )(value, *after)


def join_kernel(picks, *refs):
    for pick, out in zip(picks, refs[-len(picks) :]):
        for target, (source, *entry) in enumerate(pick):
            out[target] = refs[source][entry[0]] if entry else refs[source][...]


def join(name, values, picks, shape, after=(), flops=0):
    return pl.pallas_call(
        functools.partial(join_kernel, picks),
        out_shape=[jax.ShapeDtypeStruct((len(pick),) + shape, values[0].dtype) for pick in picks],
        in_specs=[VMEM] * len(values) + [ANY] * len(after),
        out_specs=[VMEM] * len(picks),
        compiler_params=pltpu.CompilerParams(vmem_limit_bytes=2 * MIB),
        cost_estimate=pl.CostEstimate(flops=flops, bytes_accessed=2000000, transcendentals=0),
        name=name,
    )(*values, *after)


def add_lowrank(total, me, blocks, places, tokens):
    for block, owners in zip(blocks, places):
        depth = block.shape[-1]
        for i, k in enumerate(owners):
            start = pl.multiple_of((me[0] ^ k) * depth, depth)
            part = block[i] if len(block.shape) == 3 else block[...]
            total += lax.dot_general(part, tokens[:, pl.ds(start, depth)], NT, preferred_element_type=jnp.float32)
    return total


def lowrank_kernel(places, me, tokens, *refs):
    blocks, out = refs[: len(places)], refs[-1]
    before = refs[len(places)][...] if len(refs) > len(places) + 1 else jnp.zeros(out.shape, jnp.float32)
    out[...] = add_lowrank(before, me, blocks, places, tokens)


def partial_lowrank(name, me, tokens, blocks, places, before=()):
    return pl.pallas_call(
        functools.partial(lowrank_kernel, places),
        out_shape=jax.ShapeDtypeStruct((blocks[0].shape[-2], tokens.shape[0]), jnp.float32),
        in_specs=[SMEM] + [VMEM] * (1 + len(blocks) + len(before)),
        out_specs=VMEM,
        compiler_params=pltpu.CompilerParams(vmem_limit_bytes=2 * MIB),
        cost_estimate=pl.CostEstimate(flops=100000000, bytes_accessed=2000000, transcendentals=0),
        name=name,
    )(me, tokens, *blocks, *before)


def grads_kernel(owners, places, me, tokens, *refs):
    blocks = refs[: len(places)]
    before, cotangent, mask = refs[len(places) : len(places) + 3]
    outs, grads = refs[-1 - len(owners) : -1], refs[-1]
    total = add_lowrank(before[...], me, blocks, places, tokens)
    rank = total.shape[0]
    lowrank = total.astype(jnp.bfloat16) * mask[...].astype(jnp.bfloat16)
    turned = jnp.dot(lowrank, cotangent[...], preferred_element_type=jnp.float32)
    grads[...] = turned.T
    pack = LANES // rank
    share = outs[0].shape[1]
    for out, ks in zip(outs, owners):
        for i, k in enumerate(ks):
            start = pl.multiple_of((me[0] ^ k) * (share * pack), share * pack)
            for q in range(pack):
                rows = grads[pl.ds(start + q, share, stride=pack), :]
                out[i, :, q * rank : (q + 1) * rank] = rows.astype(jnp.bfloat16)


def packed_grads(me, owners, tokens, blocks, places, before, cotangent, mask):
    rank, width = blocks[0].shape[-2], cotangent.shape[1]
    share = width * rank // LANES // sum(len(ks) for ks in owners)
    return pl.pallas_call(
        functools.partial(grads_kernel, owners, places),
        out_shape=[jax.ShapeDtypeStruct((len(ks), share, LANES), jnp.bfloat16) for ks in owners],
        in_specs=[SMEM] + [VMEM] * (len(blocks) + 4),
        out_specs=[VMEM] * len(owners),
        scratch_shapes=[pltpu.VMEM((width, rank), jnp.float32)],
        compiler_params=pltpu.CompilerParams(vmem_limit_bytes=6 * MIB),
        cost_estimate=pl.CostEstimate(flops=100000000, bytes_accessed=2000000, transcendentals=0),
        name="grads",
    )(me, tokens, *blocks, before, cotangent, mask)


def features_kernel(places, count, me, *refs):
    arrays, weights = refs[:count], refs[count]
    keep, send, x, left, total = refs[-5:]
    n = len(places)
    share = arrays[0].shape[1]
    pitch = x.shape[1] // n
    for k, (source, entry) in enumerate(places):
        rows = arrays[source][entry]
        place = pl.multiple_of((me[0] ^ k) * pitch, pitch)
        for h in range(x.shape[0]):
            x[h, pl.ds(place, share), :] = rows[:, h * 128 : (h + 1) * 128].astype(jnp.float32)
    for j in range(share):
        for h in range(x.shape[0]):
            at = j * LANES + h * 128
            left[:, at : at + 128] = x[h, pl.ds(j, n, stride=pitch), :].astype(jnp.bfloat16)
    total[...] = jnp.dot(left[...], weights[...], preferred_element_type=jnp.float32)
    part = keep.shape[1]
    mine = pl.multiple_of((me[0] & 1) * part, part)
    partner = pl.multiple_of((1 - (me[0] & 1)) * part, part)
    keep[...] = total[:, pl.ds(mine, part)]
    send[...] = total[:, pl.ds(partner, part)].astype(jnp.bfloat16)


def partial_features(me, arrays, places, projection):
    n = len(places)
    share = arrays[0].shape[1]
    depth, width = projection.shape
    half = (n, width // 2)
    return pl.pallas_call(
        functools.partial(features_kernel, places, len(arrays)),
        out_shape=[jax.ShapeDtypeStruct(half, jnp.float32), jax.ShapeDtypeStruct(half, jnp.bfloat16)],
        in_specs=[SMEM] + [VMEM] * (len(arrays) + 1),
        out_specs=[VMEM, VMEM],
        scratch_shapes=[
            pltpu.VMEM((LANES // 128, n * max(share, 8), 128), jnp.float32),
            pltpu.VMEM((n, depth), jnp.bfloat16),
            pltpu.VMEM((n, width), jnp.float32),
        ],
        compiler_params=pltpu.CompilerParams(vmem_limit_bytes=4 * MIB),
        cost_estimate=pl.CostEstimate(flops=600000000, bytes_accessed=34000000, transcendentals=0),
        name="features",
    )(me, *arrays, in_vmem(projection))


def scores_kernel(me, targets, partner_targets, kept, *refs):
    mine, send = refs[-2:]
    features = kept[...]
    for arrived in refs[:-2]:
        features += arrived[...].astype(jnp.float32)
    count, half = features.shape
    start = pl.multiple_of((me[0] & 1) * half, half)
    high = lax.Precision.HIGHEST
    ones = jnp.ones((targets.shape[0], half), jnp.float32)
    squares = lax.dot_general(ones, features * features, NT, precision=high, preferred_element_type=jnp.float32)
    rest = jnp.zeros((targets.shape[0], mine.shape[1] - 2 * count), jnp.float32)
    for source, out in ((targets, mine), (partner_targets, send)):
        scale = lax.rsqrt(jnp.sum(source[...] * source[...], axis=1, keepdims=True) / PDIM + 1e-06)
        dots = lax.dot_general(
            source[:, pl.ds(start, half)], features, NT, precision=high, preferred_element_type=jnp.float32
        )
        parts = [dots * scale, squares] + ([rest] if rest.shape[1] else [])
        out[...] = jnp.concatenate(parts, axis=1)


def partial_scores(me, targets, partner_targets, kept, arrived):
    shape = jax.ShapeDtypeStruct((targets.shape[0], 128), jnp.float32)
    return pl.pallas_call(
        scores_kernel,
        out_shape=[shape, shape],
        in_specs=[SMEM] + [VMEM] * (3 + len(arrived)),
        out_specs=[VMEM, VMEM],
        compiler_params=pltpu.CompilerParams(vmem_limit_bytes=6 * MIB),
        name="partial_scores",
    )(me, targets, partner_targets, kept, *arrived)


def body(tokens, cotangent, response_loss_mask, adapter_down_weight, projection, targets):
    n = lax.axis_size("shard")
    far = n // NEAR
    me = lax.axis_index("shard").astype(jnp.int32).reshape(1)
    block = adapter_down_weight
    bits = [1 << i for i in range(n.bit_length() - 1)]

    whole = [(tokens, 0, tokens.shape[0]), (cotangent, 0, cotangent.shape[0])]
    whole += [(response_loss_mask.reshape(1, -1), 0, 1), (targets, 0, targets.shape[0])]
    tokens, cotangent, mask, targets = load("load_1", whole, (me,))
    column = [block] + [swap(block, NEAR * d, n) for d in range(1, far)]
    (column,) = join("join_blocks", column, [[(d,) for d in range(far)]], block.shape, (mask,))
    places = [[NEAR * d + k for d in range(far)] for k in range(NEAR)]
    total = partial_lowrank("lowrank_1", me, tokens, [column], places[:1])
    across = hold("hold", swap(column, 2, n), (total,))
    total = partial_lowrank("lowrank_2", me, tokens, [swap(column, 1, n), across], places[1:3], (total,))

    stages = [bits[i : i + 2] for i in range(2, len(bits), 2)] + [bits[:2]]
    left = span([b for stage in stages[1:] for b in stage])
    moves = span(stages[0])
    owners = [[m ^ r for r in left] for m in moves]
    rows = packed_grads(me, owners, tokens, [swap(across, 1, n)], places[3:], total, cotangent, mask)
    rows = list(rows)
    rows[1] = hold("hold_rows", rows[1], (), HIDE)
    arrays = [rows[0]] + [swap(array, m, n) for array, m in zip(rows[1:], moves[1:])]
    held = {(m, r): (a, i) for a, m in enumerate(moves) for i, r in enumerate(left)}
    for number, stage in enumerate(stages[1:]):
        moves, left = span(stage), span([b for later in stages[number + 2 :] for b in later])
        pairs = [[(src, r ^ m) for src in sorted({s for s, _ in held}) for r in left] for m in moves]
        picks = [[held[pair] for pair in group] for group in pairs[1:]]
        sent = join(f"join_rows_{number}", arrays, picks, rows[0].shape[1:])
        kept = {pair: held[pair] for pair in pairs[0]}
        for m, group, array in zip(moves[1:], pairs[1:], sent):
            kept.update({(src ^ m, r ^ m): (len(arrays), i) for i, (src, r) in enumerate(group)})
            arrays.append(swap(array, m, n))
        held = kept
    partner_targets = swap(targets, 1, n)

    places = [held[k, 0] for k in range(n)]
    kept, send = partial_features(me, arrays, places, projection)
    kept = kept + swap(send, 1, n).astype(jnp.float32)
    for stage in [bits[1:3]] + [[bit] for bit in bits[3:]]:
        half = kept.astype(jnp.bfloat16)
        arrived = [swap(half, m, n) for m in span(stage)[1:]]
        if bits[-1] not in stage:
            kept = kept + sum(value.astype(jnp.float32) for value in arrived)
    mine, send = partial_scores(me, targets, partner_targets, kept, arrived)
    total = mine + swap(send, 1, n)
    scale = lax.rsqrt(total[:, n : 2 * n] / PDIM + 1e-06)
    return (total[:, :n] * scale / PDIM).T


def solution(mesh):
    in_specs = (
        P(("groups", "shard"), None),
        P(("groups", "shard"), None),
        P(("groups", "shard")),
        P(None, "shard"),
        P("shard", None),
        P(("groups", "shard"), None),
    )
    out_specs = P("groups", "shard")
    return jax.shard_map(body, mesh=mesh, in_specs=in_specs, out_specs=out_specs, check_vma=False)
```

profile of v0, /device:TPU:0, one launch (start us, length us, event | category | flops | bytes accessed | tf_op | source)
XLA Modules:
  0.0 54.5 jit_solution(594440602407208122)
XLA Ops:
  0.0 3.0 %collective-permute-start.1 = (bf16[64,512]{1,0:T(8,128)(2,1)}, bf16[64,512]{1,0:T(8,128)(2,1)S(1)}, u32[]{:S(2)}, u32[]{:S(2)}) collective-permute-start(bf16[64,512]{1,0:T(8,128)(2,1)} %refs_0_.3), channel_id=1, source_target_pairs={{0,4},{1,5},{2,6},{3,7},{4,0},{5,1},{6,2},{7,3},{8,12},{9,13},{10,... | collective-permute-start | bytes 196616 | tf_op jit(solution)/shard_map/ppermute | solution.py:23
  3.0 2.6 %collective-permute-start.2 = (bf16[64,512]{1,0:T(8,128)(2,1)}, bf16[64,512]{1,0:T(8,128)(2,1)S(1)}, u32[]{:S(2)}, u32[]{:S(2)}) collective-permute-start(bf16[64,512]{1,0:T(8,128)(2,1)} %refs_0_.3), channel_id=1, source_target_pairs={{0,8},{1,9},{2,10},{3,11},{4,12},{5,13},{6,14},{7,15},{8,0},{9,1},... | collective-permute-start | bytes 196616 | tf_op jit(solution)/shard_map/ppermute | solution.py:23
  5.6 2.4 %load_1.1 = (bf16[256,8192]{1,0:T(8,128)(2,1)S(1)}, bf16[256,1024]{1,0:T(8,128)(2,1)S(1)}, s32[1,256]{1,0:T(1,128)S(1)}, f32[8,4096]{1,0:T(8,128)S(1)}) custom-call(bf16[256,8192]{1,0:T(8,128)(2,1)} %refs_0_.2, bf16[256,1024]{1,0:T(8,128)(2,1)} %refs_1_.1, s32[1,256]{1,0:T(1,128)} %bitcast.6, f32[8,4096]{1,0:T(8,128)} %refs_3_.1, s32[1]{0:T(128)} %bitcast.refs_4_.me), custom_call_target="tpu_custom_call" | custom-call | bytes 9701376 | tf_op jit(solution)/shard_map/load_1/pallas_call | solution.py:59
  8.0 2.5 %collective-permute-done.2.refs_2_ = bf16[64,512]{1,0:T(8,128)(2,1)S(1)} collective-permute-done((bf16[64,512]{1,0:T(8,128)(2,1)}, bf16[64,512]{1,0:T(8,128)(2,1)S(1)}, u32[]{:S(2)}, u32[]{:S(2)}) %collective-permute-start.2) | collective-permute-done | bytes 65568 | tf_op jit(solution)/shard_map/ppermute | solution.py:23
  10.5 1.4 %collective-permute-done.3.refs_3_ = bf16[64,512]{1,0:T(8,128)(2,1)S(1)} collective-permute-done((bf16[64,512]{1,0:T(8,128)(2,1)}, bf16[64,512]{1,0:T(8,128)(2,1)S(1)}, u32[]{:S(2)}, u32[]{:S(2)}) %collective-permute-start.3) | collective-permute-done | bytes 65568 | tf_op jit(solution)/shard_map/ppermute | solution.py:23
  11.9 1.6 %collective-permute-start.4 = (bf16[4,64,512]{2,1,0:T(8,128)(2,1)S(1)}, bf16[4,64,512]{2,1,0:T(8,128)(2,1)S(1)}, u32[]{:S(2)}, u32[]{:S(2)}) collective-permute-start(bf16[4,64,512]{2,1,0:T(8,128)(2,1)S(1)} %join_blocks.1.refs_0_), channel_id=1, source_target_pairs={{0,2},{1,3},{2,0},{3,1},{4,6},{5,7},{6,4},{7,5},{8,10},{9,11},{10,... | collective-permute-start | bytes 786440 | tf_op jit(solution)/shard_map/ppermute | solution.py:23
  14.0 4.4 %collective-permute-done.4.refs_0_ = bf16[4,64,512]{2,1,0:T(8,128)(2,1)S(1)} collective-permute-done((bf16[4,64,512]{2,1,0:T(8,128)(2,1)S(1)}, bf16[4,64,512]{2,1,0:T(8,128)(2,1)S(1)}, u32[]{:S(2)}, u32[]{:S(2)}) %collective-permute-start.4) | collective-permute-done | bytes 262176 | tf_op jit(solution)/shard_map/ppermute | solution.py:23
  20.0 1.0 %grads.1 = (bf16[4,16,256]{2,1,0:T(8,128)(2,1)S(1)}, bf16[4,16,256]{2,1,0:T(8,128)(2,1)S(1)}, bf16[4,16,256]{2,1,0:T(8,128)(2,1)S(1)}, bf16[4,16,256]{2,1,0:T(8,128)(2,1)S(1)}) custom-call(s32[1]{0:T(128)} %bitcast.refs_4_.me, bf16[256,8192]{1,0:T(8,128)(2,1)S(1)} %get-tuple-element.21.tokens, bf16[4,64,512]{2,1,0:T(8,128)(2,1)S(1)} %collective-permute-done.5.refs_0_, ...), custom_call_target="tpu_custom_call" | custom-call | flops 100000000 | bytes 2000000 | tf_op jit(solution)/shard_map/grads/pallas_call | solution.py:152
  21.8 1.6 %collective-permute-start.8 = (bf16[4,16,256]{2,1,0:T(8,128)(2,1)S(1)}, bf16[4,16,256]{2,1,0:T(8,128)(2,1)S(1)}, u32[]{:S(2)}, u32[]{:S(2)}) collective-permute-start(bf16[4,16,256]{2,1,0:T(8,128)(2,1)S(1)} %get-tuple-element.26), channel_id=1, source_target_pairs={{0,8},{1,9},{2,10},{3,11},{4,12},{5,13},{6,14},{7,15},{8,0},{9,1},... | collective-permute-start | bytes 98312 | tf_op jit(solution)/shard_map/ppermute | solution.py:23
  23.4 2.1 %collective-permute-start.9 = (bf16[4,16,256]{2,1,0:T(8,128)(2,1)S(1)}, bf16[4,16,256]{2,1,0:T(8,128)(2,1)S(1)}, u32[]{:S(2)}, u32[]{:S(2)}) collective-permute-start(bf16[4,16,256]{2,1,0:T(8,128)(2,1)S(1)} %get-tuple-element.27), channel_id=1, source_target_pairs={{0,12},{1,13},{2,14},{3,15},{4,8},{5,9},{6,10},{7,11},{8,4},{9,5},... | collective-permute-start | bytes 98312 | tf_op jit(solution)/shard_map/ppermute | solution.py:23
  25.5 1.2 %collective-permute-done.8.refs_2_ = bf16[4,16,256]{2,1,0:T(8,128)(2,1)S(1)} collective-permute-done((bf16[4,16,256]{2,1,0:T(8,128)(2,1)S(1)}, bf16[4,16,256]{2,1,0:T(8,128)(2,1)S(1)}, u32[]{:S(2)}, u32[]{:S(2)}) %collective-permute-start.8) | collective-permute-done | bytes 32800 | tf_op jit(solution)/shard_map/ppermute | solution.py:23
  26.7 2.4 %collective-permute-done.9.refs_3_ = bf16[4,16,256]{2,1,0:T(8,128)(2,1)S(1)} collective-permute-done((bf16[4,16,256]{2,1,0:T(8,128)(2,1)S(1)}, bf16[4,16,256]{2,1,0:T(8,128)(2,1)S(1)}, u32[]{:S(2)}, u32[]{:S(2)}) %collective-permute-start.9) | collective-permute-done | bytes 32800 | tf_op jit(solution)/shard_map/ppermute | solution.py:23
  29.2 1.6 %collective-permute-start.11 = (bf16[4,16,256]{2,1,0:T(8,128)(2,1)S(1)}, bf16[4,16,256]{2,1,0:T(8,128)(2,1)S(1)}, u32[]{:S(2)}, u32[]{:S(2)}) collective-permute-start(bf16[4,16,256]{2,1,0:T(8,128)(2,1)S(1)} %get-tuple-element.29), channel_id=1, source_target_pairs={{0,2},{1,3},{2,0},{3,1},{4,6},{5,7},{6,4},{7,5},{8,10},{9,11},{10,... | collective-permute-start | bytes 98312 | tf_op jit(solution)/shard_map/ppermute | solution.py:23
  31.0 2.1 %collective-permute-done.11.refs_5_ = bf16[4,16,256]{2,1,0:T(8,128)(2,1)S(1)} collective-permute-done((bf16[4,16,256]{2,1,0:T(8,128)(2,1)S(1)}, bf16[4,16,256]{2,1,0:T(8,128)(2,1)S(1)}, u32[]{:S(2)}, u32[]{:S(2)}) %collective-permute-start.11) | collective-permute-done | bytes 32800 | tf_op jit(solution)/shard_map/ppermute | solution.py:23
  33.2 0.9 %collective-permute-done.12.refs_6_ = bf16[4,16,256]{2,1,0:T(8,128)(2,1)S(1)} collective-permute-done((bf16[4,16,256]{2,1,0:T(8,128)(2,1)S(1)}, bf16[4,16,256]{2,1,0:T(8,128)(2,1)S(1)}, u32[]{:S(2)}, u32[]{:S(2)}) %collective-permute-start.12) | collective-permute-done | bytes 32800 | tf_op jit(solution)/shard_map/ppermute | solution.py:23
  34.2 4.5 %features.1 = (f32[16,2048]{1,0:T(8,128)S(1)}, bf16[16,2048]{1,0:T(8,128)(2,1)S(1)}) custom-call(s32[1]{0:T(128)} %bitcast.refs_4_.me, bf16[4,16,256]{2,1,0:T(8,128)(2,1)S(1)} %get-tuple-element.24.refs_0_, bf16[4,16,256]{2,1,0:T(8,128)(2,1)S(1)} %collective-permute-done.7.refs_1_, bf16[4,16,256]{2,1,0:T(8,128)(2,1)S(1)} %collective-permute-done.8.refs_2_, ...), custom_call_target="tpu_custom_call" | custom-call | flops 600000000 | bytes 34000000 | tf_op jit(solution)/shard_map/features/pallas_call | solution.py:192
  38.9 1.1 %collective-permute-done.13 = bf16[16,2048]{1,0:T(8,128)(2,1)S(1)} collective-permute-done((bf16[16,2048]{1,0:T(8,128)(2,1)S(1)}, bf16[16,2048]{1,0:T(8,128)(2,1)S(1)}, u32[]{:S(2)}, u32[]{:S(2)}) %collective-permute-start.13) | collective-permute-done | bytes 65568 | tf_op jit(solution)/shard_map/ppermute | solution.py:23
  40.0 0.9 %collective-permute-start.14 = (bf16[16,2048]{1,0:T(8,128)(2,1)S(1)}, bf16[16,2048]{1,0:T(8,128)(2,1)S(1)}, u32[]{:S(2)}, u32[]{:S(2)}) collective-permute-start(bf16[16,2048]{1,0:T(8,128)(2,1)S(1)} %fusion), channel_id=1, source_target_pairs={{0,2},{1,3},{2,0},{3,1},{4,6},{5,7},{6,4},{7,5},{8,10},{9,11},{10,... | collective-permute-start | bytes 196616 | tf_op jit(solution)/shard_map/ppermute | solution.py:23
  40.9 2.6 %collective-permute-start.16 = (bf16[16,2048]{1,0:T(8,128)(2,1)S(1)}, bf16[16,2048]{1,0:T(8,128)(2,1)S(1)}, u32[]{:S(2)}, u32[]{:S(2)}) collective-permute-start(bf16[16,2048]{1,0:T(8,128)(2,1)S(1)} %fusion), channel_id=1, source_target_pairs={{0,6},{1,7},{2,4},{3,5},{4,2},{5,3},{6,0},{7,1},{8,14},{9,15},{10,... | collective-permute-start | bytes 196616 | tf_op jit(solution)/shard_map/ppermute | solution.py:23
  44.3 1.2 %collective-permute-done.15 = bf16[16,2048]{1,0:T(8,128)(2,1)S(1)} collective-permute-done((bf16[16,2048]{1,0:T(8,128)(2,1)S(1)}, bf16[16,2048]{1,0:T(8,128)(2,1)S(1)}, u32[]{:S(2)}, u32[]{:S(2)}) %collective-permute-start.15) | collective-permute-done | bytes 65568 | tf_op jit(solution)/shard_map/ppermute | solution.py:23
  45.5 1.3 %collective-permute-done.16 = bf16[16,2048]{1,0:T(8,128)(2,1)S(1)} collective-permute-done((bf16[16,2048]{1,0:T(8,128)(2,1)S(1)}, bf16[16,2048]{1,0:T(8,128)(2,1)S(1)}, u32[]{:S(2)}, u32[]{:S(2)}) %collective-permute-start.16) | collective-permute-done | bytes 65568 | tf_op jit(solution)/shard_map/ppermute | solution.py:23
  46.8 2.0 %collective-permute-start.17 = (bf16[16,2048]{1,0:T(8,128)(2,1)S(1)}, bf16[16,2048]{1,0:T(8,128)(2,1)S(1)}, u32[]{:S(2)}, u32[]{:S(2)}) collective-permute-start(bf16[16,2048]{1,0:T(8,128)(2,1)S(1)} %get-tuple-element.35), channel_id=1, source_target_pairs={{0,8},{1,9},{2,10},{3,11},{4,12},{5,13},{6,14},{7,15},{8,0},{9,1},... | collective-permute-start | bytes 196616 | tf_op jit(solution)/shard_map/ppermute | solution.py:23
  48.8 3.2 %collective-permute-done.17.refs_0_ = bf16[16,2048]{1,0:T(8,128)(2,1)S(1)} collective-permute-done((bf16[16,2048]{1,0:T(8,128)(2,1)S(1)}, bf16[16,2048]{1,0:T(8,128)(2,1)S(1)}, u32[]{:S(2)}, u32[]{:S(2)}) %collective-permute-start.17) | collective-permute-done | bytes 65568 | tf_op jit(solution)/shard_map/ppermute | solution.py:23
  52.6 1.2 %collective-permute-done.18 = f32[8,128]{1,0:T(8,128)S(1)} collective-permute-done((f32[8,128]{1,0:T(8,128)S(1)}, f32[8,128]{1,0:T(8,128)S(1)}, u32[]{:S(2)}, u32[]{:S(2)}) %collective-permute-start.18) | collective-permute-done | bytes 4128 | tf_op jit(solution)/shard_map/ppermute | solution.py:23
  (47 shorter events, 5.4 us)
Async XLA Ops:
  0.0 8.0 %collective-permute-start.1 = (bf16[64,512]{1,0:T(8,128)(2,1)}, bf16[64,512]{1,0:T(8,128)(2,1)S(1)}, u32[]{:S(2)}, u32[]{:S(2)}) collective-permute-start(bf16[64,512]{1,0:T(8,128)(2,1)} %refs_0_.3), channel_id=1, source_target_pairs={{0,4},{1,5},{2,6},{3,7},{4,0},{5,1},{6,2},{7,3},{8,12},{9,13},{10,... | collective-permute-start | bytes 196616 | tf_op jit(solution)/shard_map/ppermute | solution.py:23
  3.0 7.5 %collective-permute-start.2 = (bf16[64,512]{1,0:T(8,128)(2,1)}, bf16[64,512]{1,0:T(8,128)(2,1)S(1)}, u32[]{:S(2)}, u32[]{:S(2)}) collective-permute-start(bf16[64,512]{1,0:T(8,128)(2,1)} %refs_0_.3), channel_id=1, source_target_pairs={{0,8},{1,9},{2,10},{3,11},{4,12},{5,13},{6,14},{7,15},{8,0},{9,1},... | collective-permute-start | bytes 196616 | tf_op jit(solution)/shard_map/ppermute | solution.py:23
  5.6 6.3 %collective-permute-start.3 = (bf16[64,512]{1,0:T(8,128)(2,1)}, bf16[64,512]{1,0:T(8,128)(2,1)S(1)}, u32[]{:S(2)}, u32[]{:S(2)}) collective-permute-start(bf16[64,512]{1,0:T(8,128)(2,1)} %refs_0_.3), channel_id=1, source_target_pairs={{0,12},{1,13},{2,14},{3,15},{4,8},{5,9},{6,10},{7,11},{8,4},{9,5},... | collective-permute-start | bytes 196616 | tf_op jit(solution)/shard_map/ppermute | solution.py:23
  11.9 6.5 %collective-permute-start.4 = (bf16[4,64,512]{2,1,0:T(8,128)(2,1)S(1)}, bf16[4,64,512]{2,1,0:T(8,128)(2,1)S(1)}, u32[]{:S(2)}, u32[]{:S(2)}) collective-permute-start(bf16[4,64,512]{2,1,0:T(8,128)(2,1)S(1)} %join_blocks.1.refs_0_), channel_id=1, source_target_pairs={{0,2},{1,3},{2,0},{3,1},{4,6},{5,7},{6,4},{7,5},{8,10},{9,11},{10,... | collective-permute-start | bytes 786440 | tf_op jit(solution)/shard_map/ppermute | solution.py:23
  13.5 4.9 %collective-permute-start.6 = (bf16[4,64,512]{2,1,0:T(8,128)(2,1)S(1)}, bf16[4,64,512]{2,1,0:T(8,128)(2,1)S(1)}, u32[]{:S(2)}, u32[]{:S(2)}) collective-permute-start(bf16[4,64,512]{2,1,0:T(8,128)(2,1)S(1)} %join_blocks.1.refs_0_), channel_id=1, source_target_pairs={{0,1},{1,0},{2,3},{3,2},{4,5},{5,4},{6,7},{7,6},{8,9},{9,8},{10,11... | collective-permute-start | bytes 786440 | tf_op jit(solution)/shard_map/ppermute | solution.py:23
  18.4 1.5 %collective-permute-start.5 = (bf16[4,64,512]{2,1,0:T(8,128)(2,1)S(1)}, bf16[4,64,512]{2,1,0:T(8,128)(2,1)S(1)}, u32[]{:S(2)}, u32[]{:S(2)}) collective-permute-start(bf16[4,64,512]{2,1,0:T(8,128)(2,1)S(1)} %hold.1.refs_1_), channel_id=1, source_target_pairs={{0,1},{1,0},{2,3},{3,2},{4,5},{5,4},{6,7},{7,6},{8,9},{9,8},{10,11... | collective-permute-start | bytes 786440 | tf_op jit(solution)/shard_map/ppermute | solution.py:23
  20.9 13.2 %slice-start = ((s8[33554432]{0:T(1024)(128)(4,1)}), s8[4194304]{0:T(1024)(128)(4,1)S(1)}, s32[]{:S(2)}) async-start(s8[33554432]{0:T(1024)(128)(4,1)} %bitcast.4), calls=%async_computation | async-start | bytes 8388608
  20.9 13.2 %slice-start.1 = ((s8[33554432]{0:T(1024)(128)(4,1)}), s8[4194304]{0:T(1024)(128)(4,1)S(1)}, s32[]{:S(2)}) async-start(s8[33554432]{0:T(1024)(128)(4,1)} %bitcast.4), calls=%async_computation.1 | async-start | bytes 8388608
  20.9 13.2 %slice-start.2 = ((s8[33554432]{0:T(1024)(128)(4,1)}), s8[4194304]{0:T(1024)(128)(4,1)S(1)}, s32[]{:S(2)}) async-start(s8[33554432]{0:T(1024)(128)(4,1)} %bitcast.4), calls=%async_computation.2 | async-start | bytes 8388608
  21.0 13.2 %slice-start.3 = ((s8[33554432]{0:T(1024)(128)(4,1)}), s8[4194304]{0:T(1024)(128)(4,1)S(1)}, s32[]{:S(2)}) async-start(s8[33554432]{0:T(1024)(128)(4,1)} %bitcast.4), calls=%async_computation.3 | async-start | bytes 8388608
  21.0 13.2 %slice-start.4 = ((s8[33554432]{0:T(1024)(128)(4,1)}), s8[4194304]{0:T(1024)(128)(4,1)S(1)}, s32[]{:S(2)}) async-start(s8[33554432]{0:T(1024)(128)(4,1)} %bitcast.4), calls=%async_computation.4 | async-start | bytes 8388608
  21.0 4.5 %collective-permute-start.7 = (bf16[4,16,256]{2,1,0:T(8,128)(2,1)S(1)}, bf16[4,16,256]{2,1,0:T(8,128)(2,1)S(1)}, u32[]{:S(2)}, u32[]{:S(2)}) collective-permute-start(bf16[4,16,256]{2,1,0:T(8,128)(2,1)S(1)} %hold_rows.1), channel_id=1, source_target_pairs={{0,4},{1,5},{2,6},{3,7},{4,0},{5,1},{6,2},{7,3},{8,12},{9,13},{10,... | collective-permute-start | bytes 98312 | tf_op jit(solution)/shard_map/ppermute | solution.py:23
  21.8 4.9 %collective-permute-start.8 = (bf16[4,16,256]{2,1,0:T(8,128)(2,1)S(1)}, bf16[4,16,256]{2,1,0:T(8,128)(2,1)S(1)}, u32[]{:S(2)}, u32[]{:S(2)}) collective-permute-start(bf16[4,16,256]{2,1,0:T(8,128)(2,1)S(1)} %get-tuple-element.26), channel_id=1, source_target_pairs={{0,8},{1,9},{2,10},{3,11},{4,12},{5,13},{6,14},{7,15},{8,0},{9,1},... | collective-permute-start | bytes 98312 | tf_op jit(solution)/shard_map/ppermute | solution.py:23
  23.4 5.7 %collective-permute-start.9 = (bf16[4,16,256]{2,1,0:T(8,128)(2,1)S(1)}, bf16[4,16,256]{2,1,0:T(8,128)(2,1)S(1)}, u32[]{:S(2)}, u32[]{:S(2)}) collective-permute-start(bf16[4,16,256]{2,1,0:T(8,128)(2,1)S(1)} %get-tuple-element.27), channel_id=1, source_target_pairs={{0,12},{1,13},{2,14},{3,15},{4,8},{5,9},{6,10},{7,11},{8,4},{9,5},... | collective-permute-start | bytes 98312 | tf_op jit(solution)/shard_map/ppermute | solution.py:23
  29.1 1.9 %collective-permute-start.10 = (bf16[4,16,256]{2,1,0:T(8,128)(2,1)S(1)}, bf16[4,16,256]{2,1,0:T(8,128)(2,1)S(1)}, u32[]{:S(2)}, u32[]{:S(2)}) collective-permute-start(bf16[4,16,256]{2,1,0:T(8,128)(2,1)S(1)} %get-tuple-element.28), channel_id=1, source_target_pairs={{0,1},{1,0},{2,3},{3,2},{4,5},{5,4},{6,7},{7,6},{8,9},{9,8},{10,11... | collective-permute-start | bytes 98312 | tf_op jit(solution)/shard_map/ppermute | solution.py:23
  29.2 4.0 %collective-permute-start.11 = (bf16[4,16,256]{2,1,0:T(8,128)(2,1)S(1)}, bf16[4,16,256]{2,1,0:T(8,128)(2,1)S(1)}, u32[]{:S(2)}, u32[]{:S(2)}) collective-permute-start(bf16[4,16,256]{2,1,0:T(8,128)(2,1)S(1)} %get-tuple-element.29), channel_id=1, source_target_pairs={{0,2},{1,3},{2,0},{3,1},{4,6},{5,7},{6,4},{7,5},{8,10},{9,11},{10,... | collective-permute-start | bytes 98312 | tf_op jit(solution)/shard_map/ppermute | solution.py:23
  30.8 3.3 %collective-permute-start.12 = (bf16[4,16,256]{2,1,0:T(8,128)(2,1)S(1)}, bf16[4,16,256]{2,1,0:T(8,128)(2,1)S(1)}, u32[]{:S(2)}, u32[]{:S(2)}) collective-permute-start(bf16[4,16,256]{2,1,0:T(8,128)(2,1)S(1)} %get-tuple-element.30), channel_id=1, source_target_pairs={{0,3},{1,2},{2,1},{3,0},{4,7},{5,6},{6,5},{7,4},{8,11},{9,10},{10,... | collective-permute-start | bytes 98312 | tf_op jit(solution)/shard_map/ppermute | solution.py:23
  38.7 1.3 %collective-permute-start.13 = (bf16[16,2048]{1,0:T(8,128)(2,1)S(1)}, bf16[16,2048]{1,0:T(8,128)(2,1)S(1)}, u32[]{:S(2)}, u32[]{:S(2)}) collective-permute-start(bf16[16,2048]{1,0:T(8,128)(2,1)S(1)} %get-tuple-element.32), channel_id=1, source_target_pairs={{0,1},{1,0},{2,3},{3,2},{4,5},{5,4},{6,7},{7,6},{8,9},{9,8},{10,11... | collective-permute-start | bytes 196616 | tf_op jit(solution)/shard_map/ppermute | solution.py:23
  40.0 4.3 %collective-permute-start.14 = (bf16[16,2048]{1,0:T(8,128)(2,1)S(1)}, bf16[16,2048]{1,0:T(8,128)(2,1)S(1)}, u32[]{:S(2)}, u32[]{:S(2)}) collective-permute-start(bf16[16,2048]{1,0:T(8,128)(2,1)S(1)} %fusion), channel_id=1, source_target_pairs={{0,2},{1,3},{2,0},{3,1},{4,6},{5,7},{6,4},{7,5},{8,10},{9,11},{10,... | collective-permute-start | bytes 196616 | tf_op jit(solution)/shard_map/ppermute | solution.py:23
  40.9 4.6 %collective-permute-start.15 = (bf16[16,2048]{1,0:T(8,128)(2,1)S(1)}, bf16[16,2048]{1,0:T(8,128)(2,1)S(1)}, u32[]{:S(2)}, u32[]{:S(2)}) collective-permute-start(bf16[16,2048]{1,0:T(8,128)(2,1)S(1)} %fusion), channel_id=1, source_target_pairs={{0,4},{1,5},{2,6},{3,7},{4,0},{5,1},{6,2},{7,3},{8,12},{9,13},{10,... | collective-permute-start | bytes 196616 | tf_op jit(solution)/shard_map/ppermute | solution.py:23
  40.9 5.9 %collective-permute-start.16 = (bf16[16,2048]{1,0:T(8,128)(2,1)S(1)}, bf16[16,2048]{1,0:T(8,128)(2,1)S(1)}, u32[]{:S(2)}, u32[]{:S(2)}) collective-permute-start(bf16[16,2048]{1,0:T(8,128)(2,1)S(1)} %fusion), channel_id=1, source_target_pairs={{0,6},{1,7},{2,4},{3,5},{4,2},{5,3},{6,0},{7,1},{8,14},{9,15},{10,... | collective-permute-start | bytes 196616 | tf_op jit(solution)/shard_map/ppermute | solution.py:23
  43.5 5.3 %collective-permute-start = (f32[8,4096]{1,0:T(8,128)S(1)}, f32[8,4096]{1,0:T(8,128)S(1)}, u32[]{:S(2)}, u32[]{:S(2)}) collective-permute-start(f32[8,4096]{1,0:T(8,128)S(1)} %get-tuple-element.20.targets), channel_id=1, source_target_pairs={{0,1},{1,0},{2,3},{3,2},{4,5},{5,4},{6,7},{7,6},{8,9},{9,8},{10,11... | collective-permute-start | bytes 393224 | tf_op jit(solution)/shard_map/ppermute | solution.py:23
  46.8 5.2 %collective-permute-start.17 = (bf16[16,2048]{1,0:T(8,128)(2,1)S(1)}, bf16[16,2048]{1,0:T(8,128)(2,1)S(1)}, u32[]{:S(2)}, u32[]{:S(2)}) collective-permute-start(bf16[16,2048]{1,0:T(8,128)(2,1)S(1)} %get-tuple-element.35), channel_id=1, source_target_pairs={{0,8},{1,9},{2,10},{3,11},{4,12},{5,13},{6,14},{7,15},{8,0},{9,1},... | collective-permute-start | bytes 196616 | tf_op jit(solution)/shard_map/ppermute | solution.py:23
  52.6 1.2 %collective-permute-start.18 = (f32[8,128]{1,0:T(8,128)S(1)}, f32[8,128]{1,0:T(8,128)S(1)}, u32[]{:S(2)}, u32[]{:S(2)}) collective-permute-start(f32[8,128]{1,0:T(8,128)S(1)} %get-tuple-element.34), channel_id=1, source_target_pairs={{0,1},{1,0},{2,3},{3,2},{4,5},{5,4},{6,7},{7,6},{8,9},{9,8},{10,11... | collective-permute-start | bytes 12296 | tf_op jit(solution)/shard_map/ppermute | solution.py:23
  (4 other events, 51.4 us)
where the time goes:
time: 54.6 us; the launch traced here: 54.5 us
  waiting for transfers between devices  24.5 us (45%)
  starting transfers between devices  19.3 us (35%)
  Pallas kernels  9.65 us (18%)
  other arithmetic  0.74 us (1%)
    ppermute x19, waiting for transfers between devices, swap(): return lax.ppermute(value, 'shard', [(s, s ^ bit) for s in range(n)])  24.5 us
    ppermute x19, starting transfers between devices, swap(): return lax.ppermute(value, 'shard', [(s, s ^ bit) for s in range(n)])  19.3 us
    pallas_call x1, Pallas kernels, partial_features(): pl.pallas_call(functools.partial(features_kernel, places, len(arrays)), o...  4.5 us
    pallas_call x1, Pallas kernels, load(): pl.pallas_call(functools.partial(load_kernel, len(parts), [start for _, s...  2.39 us
    pallas_call x2, Pallas kernels, partial_lowrank(): pl.pallas_call(functools.partial(lowrank_kernel, places), out_shape=jax.S...  1.2 us
  transfers between devices with their start and end apart: 19, of which 14 were waited for; matrix products, arithmetic and copies ran while one was open for 0% of the time, Pallas kernels for 7%

commit v1 on v0

--- a/solution.py
+++ b/solution.py
@@ -247,18 +247,27 @@
     whole = [(tokens, 0, tokens.shape[0]), (cotangent, 0, cotangent.shape[0])]
     whole += [(response_loss_mask.reshape(1, -1), 0, 1), (targets, 0, targets.shape[0])]
     tokens, cotangent, mask, targets = load("load_1", whole, (me,))
-    column = [block] + [swap(block, NEAR * d, n) for d in range(1, far)]
-    (column,) = join("join_blocks", column, [[(d,) for d in range(far)]], block.shape, (mask,))
-    places = [[NEAR * d + k for d in range(far)] for k in range(NEAR)]
-    total = partial_lowrank("lowrank_1", me, tokens, [column], places[:1])
-    across = hold("hold", swap(column, 2, n), (total,))
-    total = partial_lowrank("lowrank_2", me, tokens, [swap(column, 1, n), across], places[1:3], (total,))
+    column = list(load("load_own", [(block, 0, block.shape[0])], (me,)))
+    column += [swap(block, NEAR * d, n) for d in range(1, far)]
+    cut = far // 2
+    picks = [[(i,) for i in range(cut)]]
+    (head,) = join("join_head", column[:cut], picks, block.shape)
+    (tail,) = join("join_tail", column[cut:], picks, block.shape, (mask, head))
+    places = [[[NEAR * d + k for d in half] for half in (range(cut), range(cut, far))] for k in range(NEAR)]
+    across = [swap(head, 2, n), swap(tail, 2, n)]
+    blocks, owners = [head, tail, swap(head, 1, n), across[0]], places[0] + places[1][:1] + places[2][:1]
+    total = partial_lowrank("lowrank_1", me, tokens, blocks, owners)
+    picks = [[(a, i) for a in range(3) for i in range(cut)]]
+    (gathered,) = join("join_core", [tail] + across, picks, block.shape, (total,))
+    other = swap(gathered, 1, n)
+    total = partial_lowrank("lowrank_2", me, tokens, across[1:], places[2][1:], (total,))
+    owners = [places[1][1] + places[3][0] + places[3][1]]
 
     stages = [bits[i : i + 2] for i in range(2, len(bits), 2)] + [bits[:2]]
     left = span([b for stage in stages[1:] for b in stage])
     moves = span(stages[0])
-    owners = [[m ^ r for r in left] for m in moves]
-    rows = packed_grads(me, owners, tokens, [swap(across, 1, n)], places[3:], total, cotangent, mask)
+    targets_of = [[m ^ r for r in left] for m in moves]
+    rows = packed_grads(me, targets_of, tokens, [other], owners, total, cotangent, mask)
     rows = list(rows)
     rows[1] = hold("hold_rows", rows[1], (), HIDE)
     arrays = [rows[0]] + [swap(array, m, n) for array, m in zip(rows[1:], moves[1:])]

time: 54.6 us -> 53.9 us (0.987)
  waiting for transfers between devices: 24.5 us -> 22 us
  Pallas kernels: 9.65 us -> 10.6 us
  starting transfers between devices: 19.3 us -> 20.1 us
    ppermute x19 -> x20, waiting for transfers between devices: 24.5 us -> 22 us  [swap(): return lax.ppermute(value, 'shard', [(s, s ^ bit) for s in range(n)])]
    pallas_call x1 -> x2, Pallas kernels: 2.39 us -> 3.3 us  [load(): pl.pallas_call(functools.partial(load_kernel, len(parts), [start for _, s...]
    ppermute x19 -> x20, starting transfers between devices: 19.3 us -> 20.1 us  [swap(): return lax.ppermute(value, 'shard', [(s, s ^ bit) for s in range(n)])]
  transfers between devices with their start and end apart: 19 -> 20, of which waited for: 14 -> 13; matrix products, arithmetic and copies ran while one was open for 0% -> 0% of each run, Pallas kernels for 7% -> 8%
where the time goes in v1:
time: 53.9 us; the launch traced here: 53.8 us
  waiting for transfers between devices  22 us (41%)
  starting transfers between devices  20.1 us (37%)
  Pallas kernels  10.6 us (20%)
  other arithmetic  0.74 us (1%)
    ppermute x20, waiting for transfers between devices, swap(): return lax.ppermute(value, 'shard', [(s, s ^ bit) for s in range(n)])  22 us
    ppermute x20, starting transfers between devices, swap(): return lax.ppermute(value, 'shard', [(s, s ^ bit) for s in range(n)])  20.1 us
    pallas_call x1, Pallas kernels, partial_features(): pl.pallas_call(functools.partial(features_kernel, places, len(arrays)), o...  4.5 us
    pallas_call x2, Pallas kernels, load(): pl.pallas_call(functools.partial(load_kernel, len(parts), [start for _, s...  3.3 us
    pallas_call x1, Pallas kernels, packed_grads(): pl.pallas_call(functools.partial(grads_kernel, owners, places), out_shape...  1.12 us
  transfers between devices with their start and end apart: 20, of which 13 were waited for; matrix products, arithmetic and copies ran while one was open for 0% of the time, Pallas kernels for 8%

profile of v1, /device:TPU:0, one launch (start us, length us, event | category | flops | bytes accessed | tf_op | source)
XLA Modules:
  0.0 53.8 jit_solution(9676116855201538211)
XLA Ops:
  0.0 3.0 %collective-permute-start.3 = (bf16[64,512]{1,0:T(8,128)(2,1)}, bf16[64,512]{1,0:T(8,128)(2,1)S(1)}, u32[]{:S(2)}, u32[]{:S(2)}) collective-permute-start(bf16[64,512]{1,0:T(8,128)(2,1)} %refs_0_.3), channel_id=1, source_target_pairs={{0,4},{1,5},{2,6},{3,7},{4,0},{5,1},{6,2},{7,3},{8,12},{9,13},{10,... | collective-permute-start | bytes 196616 | tf_op jit(solution)/shard_map/ppermute | solution.py:23
  3.0 2.6 %collective-permute-start.1 = (bf16[64,512]{1,0:T(8,128)(2,1)}, bf16[64,512]{1,0:T(8,128)(2,1)S(1)}, u32[]{:S(2)}, u32[]{:S(2)}) collective-permute-start(bf16[64,512]{1,0:T(8,128)(2,1)} %refs_0_.3), channel_id=1, source_target_pairs={{0,8},{1,9},{2,10},{3,11},{4,12},{5,13},{6,14},{7,15},{8,0},{9,1},... | collective-permute-start | bytes 196616 | tf_op jit(solution)/shard_map/ppermute | solution.py:23
  5.6 0.9 %load_own.1.refs_0_ = bf16[64,512]{1,0:T(8,128)(2,1)S(1)} custom-call(bf16[64,512]{1,0:T(8,128)(2,1)} %refs_0_.3, s32[1]{0:T(128)} %bitcast.refs_4_.refs_1_.me), custom_call_target="tpu_custom_call" | custom-call | bytes 131072 | tf_op jit(solution)/shard_map/load_own/pallas_call | solution.py:59
  6.6 1.8 %collective-permute-start.4 = (bf16[2,64,512]{2,1,0:T(8,128)(2,1)S(1)}, bf16[2,64,512]{2,1,0:T(8,128)(2,1)S(1)}, u32[]{:S(2)}, u32[]{:S(2)}) collective-permute-start(bf16[2,64,512]{2,1,0:T(8,128)(2,1)S(1)} %join_head.1.refs_3_.refs_0_), channel_id=1, source_target_pairs={{0,2},{1,3},{2,0},{3,1},{4,6},{5,7},{6,4},{7,5},{8,10},{9,11},{10,... | collective-permute-start | bytes 393224 | tf_op jit(solution)/shard_map/ppermute | solution.py:23
  8.3 2.4 %load_1.1 = (bf16[256,8192]{1,0:T(8,128)(2,1)S(1)}, bf16[256,1024]{1,0:T(8,128)(2,1)S(1)}, s32[1,256]{1,0:T(1,128)S(1)}, f32[8,4096]{1,0:T(8,128)S(1)}) custom-call(bf16[256,8192]{1,0:T(8,128)(2,1)} %refs_0_.2, bf16[256,1024]{1,0:T(8,128)(2,1)} %refs_1_.1, s32[1,256]{1,0:T(1,128)} %bitcast.6, f32[8,4096]{1,0:T(8,128)} %refs_3_.1, s32[1]{0:T(128)} %bitcast.refs_4_.refs_1_.me), custom_call_target="tpu_custom_call" | custom-call | bytes 9701376 | tf_op jit(solution)/shard_map/load_1/pallas_call | solution.py:59
  10.8 1.2 %collective-permute-done.2.refs_1_ = bf16[64,512]{1,0:T(8,128)(2,1)S(1)} collective-permute-done((bf16[64,512]{1,0:T(8,128)(2,1)}, bf16[64,512]{1,0:T(8,128)(2,1)S(1)}, u32[]{:S(2)}, u32[]{:S(2)}) %collective-permute-start.2) | collective-permute-done | bytes 65568 | tf_op jit(solution)/shard_map/ppermute | solution.py:23
  11.9 1.6 %collective-permute-start.5 = (bf16[2,64,512]{2,1,0:T(8,128)(2,1)S(1)}, bf16[2,64,512]{2,1,0:T(8,128)(2,1)S(1)}, u32[]{:S(2)}, u32[]{:S(2)}) collective-permute-start(bf16[2,64,512]{2,1,0:T(8,128)(2,1)S(1)} %join_tail.1.refs_1_.refs_0_), channel_id=1, source_target_pairs={{0,2},{1,3},{2,0},{3,1},{4,6},{5,7},{6,4},{7,5},{8,10},{9,11},{10,... | collective-permute-start | bytes 393224 | tf_op jit(solution)/shard_map/ppermute | solution.py:23
  14.3 2.7 %collective-permute-done.5.refs_2_.refs_0_ = bf16[2,64,512]{2,1,0:T(8,128)(2,1)S(1)} collective-permute-done((bf16[2,64,512]{2,1,0:T(8,128)(2,1)S(1)}, bf16[2,64,512]{2,1,0:T(8,128)(2,1)S(1)}, u32[]{:S(2)}, u32[]{:S(2)}) %collective-permute-start.5) | collective-permute-done | bytes 131104 | tf_op jit(solution)/shard_map/ppermute | solution.py:23
  17.4 1.4 %collective-permute-done.7.refs_0_ = bf16[6,64,512]{2,1,0:T(8,128)(2,1)S(1)} collective-permute-done((bf16[6,64,512]{2,1,0:T(8,128)(2,1)S(1)}, bf16[6,64,512]{2,1,0:T(8,128)(2,1)S(1)}, u32[]{:S(2)}, u32[]{:S(2)}) %collective-permute-start.7) | collective-permute-done | bytes 393248 | tf_op jit(solution)/shard_map/ppermute | solution.py:23
  18.8 1.1 %grads.1 = (bf16[4,16,256]{2,1,0:T(8,128)(2,1)S(1)}, bf16[4,16,256]{2,1,0:T(8,128)(2,1)S(1)}, bf16[4,16,256]{2,1,0:T(8,128)(2,1)S(1)}, bf16[4,16,256]{2,1,0:T(8,128)(2,1)S(1)}) custom-call(s32[1]{0:T(128)} %bitcast.refs_4_.refs_1_.me, bf16[256,8192]{1,0:T(8,128)(2,1)S(1)} %get-tuple-element.21.tokens, ...), custom_call_target="tpu_custom_call" | custom-call | flops 100000000 | bytes 2000000 | tf_op jit(solution)/shard_map/grads/pallas_call | solution.py:152
  20.6 2.9 %collective-permute-start.10 = (bf16[4,16,256]{2,1,0:T(8,128)(2,1)S(1)}, bf16[4,16,256]{2,1,0:T(8,128)(2,1)S(1)}, u32[]{:S(2)}, u32[]{:S(2)}) collective-permute-start(bf16[4,16,256]{2,1,0:T(8,128)(2,1)S(1)} %get-tuple-element.27), channel_id=1, source_target_pairs={{0,12},{1,13},{2,14},{3,15},{4,8},{5,9},{6,10},{7,11},{8,4},{9,5},... | collective-permute-start | bytes 98312 | tf_op jit(solution)/shard_map/ppermute | solution.py:23
  24.0 2.3 %collective-permute-done.10.refs_3_ = bf16[4,16,256]{2,1,0:T(8,128)(2,1)S(1)} collective-permute-done((bf16[4,16,256]{2,1,0:T(8,128)(2,1)S(1)}, bf16[4,16,256]{2,1,0:T(8,128)(2,1)S(1)}, u32[]{:S(2)}, u32[]{:S(2)}) %collective-permute-start.10) | collective-permute-done | bytes 32800 | tf_op jit(solution)/shard_map/ppermute | solution.py:23
  26.3 2.0 %collective-permute-done.9.refs_2_ = bf16[4,16,256]{2,1,0:T(8,128)(2,1)S(1)} collective-permute-done((bf16[4,16,256]{2,1,0:T(8,128)(2,1)S(1)}, bf16[4,16,256]{2,1,0:T(8,128)(2,1)S(1)}, u32[]{:S(2)}, u32[]{:S(2)}) %collective-permute-start.9) | collective-permute-done | bytes 32800 | tf_op jit(solution)/shard_map/ppermute | solution.py:23
  28.4 1.4 %collective-permute-start.12 = (bf16[4,16,256]{2,1,0:T(8,128)(2,1)S(1)}, bf16[4,16,256]{2,1,0:T(8,128)(2,1)S(1)}, u32[]{:S(2)}, u32[]{:S(2)}) collective-permute-start(bf16[4,16,256]{2,1,0:T(8,128)(2,1)S(1)} %get-tuple-element.29), channel_id=1, source_target_pairs={{0,2},{1,3},{2,0},{3,1},{4,6},{5,7},{6,4},{7,5},{8,10},{9,11},{10,... | collective-permute-start | bytes 98312 | tf_op jit(solution)/shard_map/ppermute | solution.py:23
  30.3 2.1 %collective-permute-done.12.refs_5_ = bf16[4,16,256]{2,1,0:T(8,128)(2,1)S(1)} collective-permute-done((bf16[4,16,256]{2,1,0:T(8,128)(2,1)S(1)}, bf16[4,16,256]{2,1,0:T(8,128)(2,1)S(1)}, u32[]{:S(2)}, u32[]{:S(2)}) %collective-permute-start.12) | collective-permute-done | bytes 32800 | tf_op jit(solution)/shard_map/ppermute | solution.py:23
  33.3 4.5 %features.1 = (f32[16,2048]{1,0:T(8,128)S(1)}, bf16[16,2048]{1,0:T(8,128)(2,1)S(1)}) custom-call(s32[1]{0:T(128)} %bitcast.refs_4_.refs_1_.me, bf16[4,16,256]{2,1,0:T(8,128)(2,1)S(1)} %get-tuple-element.24.refs_0_, bf16[4,16,256]{2,1,0:T(8,128)(2,1)S(1)} %collective-permute-done.8.refs_1_, bf16[4,16,256]{2,1,0:T(8,128)(2,1)S(1)} %collective-permute-done.9.refs_2_, ...), custom_call_target="tpu_custom_call" | custom-call | flops 600000000 | bytes 34000000 | tf_op jit(solution)/shard_map/features/pallas_call | solution.py:192
  38.0 1.1 %collective-permute-done.14 = bf16[16,2048]{1,0:T(8,128)(2,1)S(1)} collective-permute-done((bf16[16,2048]{1,0:T(8,128)(2,1)S(1)}, bf16[16,2048]{1,0:T(8,128)(2,1)S(1)}, u32[]{:S(2)}, u32[]{:S(2)}) %collective-permute-start.14) | collective-permute-done | bytes 65568 | tf_op jit(solution)/shard_map/ppermute | solution.py:23
  39.1 1.1 %collective-permute-start.15 = (bf16[16,2048]{1,0:T(8,128)(2,1)S(1)}, bf16[16,2048]{1,0:T(8,128)(2,1)S(1)}, u32[]{:S(2)}, u32[]{:S(2)}) collective-permute-start(bf16[16,2048]{1,0:T(8,128)(2,1)S(1)} %fusion), channel_id=1, source_target_pairs={{0,2},{1,3},{2,0},{3,1},{4,6},{5,7},{6,4},{7,5},{8,10},{9,11},{10,... | collective-permute-start | bytes 196616 | tf_op jit(solution)/shard_map/ppermute | solution.py:23
  40.9 1.8 %collective-permute-start.17 = (bf16[16,2048]{1,0:T(8,128)(2,1)S(1)}, bf16[16,2048]{1,0:T(8,128)(2,1)S(1)}, u32[]{:S(2)}, u32[]{:S(2)}) collective-permute-start(bf16[16,2048]{1,0:T(8,128)(2,1)S(1)} %fusion), channel_id=1, source_target_pairs={{0,6},{1,7},{2,4},{3,5},{4,2},{5,3},{6,0},{7,1},{8,14},{9,15},{10,... | collective-permute-start | bytes 196616 | tf_op jit(solution)/shard_map/ppermute | solution.py:23
  43.4 1.4 %collective-permute-done.16 = bf16[16,2048]{1,0:T(8,128)(2,1)S(1)} collective-permute-done((bf16[16,2048]{1,0:T(8,128)(2,1)S(1)}, bf16[16,2048]{1,0:T(8,128)(2,1)S(1)}, u32[]{:S(2)}, u32[]{:S(2)}) %collective-permute-start.16) | collective-permute-done | bytes 65568 | tf_op jit(solution)/shard_map/ppermute | solution.py:23
  44.8 1.3 %collective-permute-done.17 = bf16[16,2048]{1,0:T(8,128)(2,1)S(1)} collective-permute-done((bf16[16,2048]{1,0:T(8,128)(2,1)S(1)}, bf16[16,2048]{1,0:T(8,128)(2,1)S(1)}, u32[]{:S(2)}, u32[]{:S(2)}) %collective-permute-start.17) | collective-permute-done | bytes 65568 | tf_op jit(solution)/shard_map/ppermute | solution.py:23
  46.1 1.4 %collective-permute-start.18 = (bf16[16,2048]{1,0:T(8,128)(2,1)S(1)}, bf16[16,2048]{1,0:T(8,128)(2,1)S(1)}, u32[]{:S(2)}, u32[]{:S(2)}) collective-permute-start(bf16[16,2048]{1,0:T(8,128)(2,1)S(1)} %get-tuple-element.35), channel_id=1, source_target_pairs={{0,8},{1,9},{2,10},{3,11},{4,12},{5,13},{6,14},{7,15},{8,0},{9,1},... | collective-permute-start | bytes 196616 | tf_op jit(solution)/shard_map/ppermute | solution.py:23
  47.5 3.8 %collective-permute-done.18.refs_0_ = bf16[16,2048]{1,0:T(8,128)(2,1)S(1)} collective-permute-done((bf16[16,2048]{1,0:T(8,128)(2,1)S(1)}, bf16[16,2048]{1,0:T(8,128)(2,1)S(1)}, u32[]{:S(2)}, u32[]{:S(2)}) %collective-permute-start.18) | collective-permute-done | bytes 65568 | tf_op jit(solution)/shard_map/ppermute | solution.py:23
  51.9 1.2 %collective-permute-done.19 = f32[8,128]{1,0:T(8,128)S(1)} collective-permute-done((f32[8,128]{1,0:T(8,128)S(1)}, f32[8,128]{1,0:T(8,128)S(1)}, u32[]{:S(2)}, u32[]{:S(2)}) %collective-permute-start.19) | collective-permute-done | bytes 4128 | tf_op jit(solution)/shard_map/ppermute | solution.py:23
  (49 shorter events, 6.6 us)
Async XLA Ops:
  0.0 6.5 %collective-permute-start.3 = (bf16[64,512]{1,0:T(8,128)(2,1)}, bf16[64,512]{1,0:T(8,128)(2,1)S(1)}, u32[]{:S(2)}, u32[]{:S(2)}) collective-permute-start(bf16[64,512]{1,0:T(8,128)(2,1)} %refs_0_.3), channel_id=1, source_target_pairs={{0,4},{1,5},{2,6},{3,7},{4,0},{5,1},{6,2},{7,3},{8,12},{9,13},{10,... | collective-permute-start | bytes 196616 | tf_op jit(solution)/shard_map/ppermute | solution.py:23
  3.0 7.7 %collective-permute-start.1 = (bf16[64,512]{1,0:T(8,128)(2,1)}, bf16[64,512]{1,0:T(8,128)(2,1)S(1)}, u32[]{:S(2)}, u32[]{:S(2)}) collective-permute-start(bf16[64,512]{1,0:T(8,128)(2,1)} %refs_0_.3), channel_id=1, source_target_pairs={{0,8},{1,9},{2,10},{3,11},{4,12},{5,13},{6,14},{7,15},{8,0},{9,1},... | collective-permute-start | bytes 196616 | tf_op jit(solution)/shard_map/ppermute | solution.py:23
  5.6 6.3 %collective-permute-start.2 = (bf16[64,512]{1,0:T(8,128)(2,1)}, bf16[64,512]{1,0:T(8,128)(2,1)S(1)}, u32[]{:S(2)}, u32[]{:S(2)}) collective-permute-start(bf16[64,512]{1,0:T(8,128)(2,1)} %refs_0_.3), channel_id=1, source_target_pairs={{0,12},{1,13},{2,14},{3,15},{4,8},{5,9},{6,10},{7,11},{8,4},{9,5},... | collective-permute-start | bytes 196616 | tf_op jit(solution)/shard_map/ppermute | solution.py:23
  6.6 7.0 %collective-permute-start.4 = (bf16[2,64,512]{2,1,0:T(8,128)(2,1)S(1)}, bf16[2,64,512]{2,1,0:T(8,128)(2,1)S(1)}, u32[]{:S(2)}, u32[]{:S(2)}) collective-permute-start(bf16[2,64,512]{2,1,0:T(8,128)(2,1)S(1)} %join_head.1.refs_3_.refs_0_), channel_id=1, source_target_pairs={{0,2},{1,3},{2,0},{3,1},{4,6},{5,7},{6,4},{7,5},{8,10},{9,11},{10,... | collective-permute-start | bytes 393224 | tf_op jit(solution)/shard_map/ppermute | solution.py:23
  8.3 5.2 %collective-permute-start.6 = (bf16[2,64,512]{2,1,0:T(8,128)(2,1)S(1)}, bf16[2,64,512]{2,1,0:T(8,128)(2,1)S(1)}, u32[]{:S(2)}, u32[]{:S(2)}) collective-permute-start(bf16[2,64,512]{2,1,0:T(8,128)(2,1)S(1)} %join_head.1.refs_3_.refs_0_), channel_id=1, source_target_pairs={{0,1},{1,0},{2,3},{3,2},{4,5},{5,4},{6,7},{7,6},{8,9},{9,8},{10,11... | collective-permute-start | bytes 393224 | tf_op jit(solution)/shard_map/ppermute | solution.py:23
  11.9 5.0 %collective-permute-start.5 = (bf16[2,64,512]{2,1,0:T(8,128)(2,1)S(1)}, bf16[2,64,512]{2,1,0:T(8,128)(2,1)S(1)}, u32[]{:S(2)}, u32[]{:S(2)}) collective-permute-start(bf16[2,64,512]{2,1,0:T(8,128)(2,1)S(1)} %join_tail.1.refs_1_.refs_0_), channel_id=1, source_target_pairs={{0,2},{1,3},{2,0},{3,1},{4,6},{5,7},{6,4},{7,5},{8,10},{9,11},{10,... | collective-permute-start | bytes 393224 | tf_op jit(solution)/shard_map/ppermute | solution.py:23
  17.0 1.8 %collective-permute-start.7 = (bf16[6,64,512]{2,1,0:T(8,128)(2,1)S(1)}, bf16[6,64,512]{2,1,0:T(8,128)(2,1)S(1)}, u32[]{:S(2)}, u32[]{:S(2)}) collective-permute-start(bf16[6,64,512]{2,1,0:T(8,128)(2,1)S(1)} %join_core.1), channel_id=1, source_target_pairs={{0,1},{1,0},{2,3},{3,2},{4,5},{5,4},{6,7},{7,6},{8,9},{9,8},{10,11... | collective-permute-start | bytes 1179656 | tf_op jit(solution)/shard_map/ppermute | solution.py:23
  19.9 13.3 %slice-start = ((s8[33554432]{0:T(1024)(128)(4,1)}), s8[4194304]{0:T(1024)(128)(4,1)S(1)}, s32[]{:S(2)}) async-start(s8[33554432]{0:T(1024)(128)(4,1)} %bitcast.4), calls=%async_computation | async-start | bytes 8388608
  19.9 13.3 %slice-start.1 = ((s8[33554432]{0:T(1024)(128)(4,1)}), s8[4194304]{0:T(1024)(128)(4,1)S(1)}, s32[]{:S(2)}) async-start(s8[33554432]{0:T(1024)(128)(4,1)} %bitcast.4), calls=%async_computation.1 | async-start | bytes 8388608
  19.9 13.3 %slice-start.2 = ((s8[33554432]{0:T(1024)(128)(4,1)}), s8[4194304]{0:T(1024)(128)(4,1)S(1)}, s32[]{:S(2)}) async-start(s8[33554432]{0:T(1024)(128)(4,1)} %bitcast.4), calls=%async_computation.2 | async-start | bytes 8388608
  19.9 13.3 %slice-start.3 = ((s8[33554432]{0:T(1024)(128)(4,1)}), s8[4194304]{0:T(1024)(128)(4,1)S(1)}, s32[]{:S(2)}) async-start(s8[33554432]{0:T(1024)(128)(4,1)} %bitcast.4), calls=%async_computation.3 | async-start | bytes 8388608
  20.0 4.0 %collective-permute-start.8 = (bf16[4,16,256]{2,1,0:T(8,128)(2,1)S(1)}, bf16[4,16,256]{2,1,0:T(8,128)(2,1)S(1)}, u32[]{:S(2)}, u32[]{:S(2)}) collective-permute-start(bf16[4,16,256]{2,1,0:T(8,128)(2,1)S(1)} %hold_rows.1), channel_id=1, source_target_pairs={{0,4},{1,5},{2,6},{3,7},{4,0},{5,1},{6,2},{7,3},{8,12},{9,13},{10,... | collective-permute-start | bytes 98312 | tf_op jit(solution)/shard_map/ppermute | solution.py:23
  20.6 5.7 %collective-permute-start.10 = (bf16[4,16,256]{2,1,0:T(8,128)(2,1)S(1)}, bf16[4,16,256]{2,1,0:T(8,128)(2,1)S(1)}, u32[]{:S(2)}, u32[]{:S(2)}) collective-permute-start(bf16[4,16,256]{2,1,0:T(8,128)(2,1)S(1)} %get-tuple-element.27), channel_id=1, source_target_pairs={{0,12},{1,13},{2,14},{3,15},{4,8},{5,9},{6,10},{7,11},{8,4},{9,5},... | collective-permute-start | bytes 98312 | tf_op jit(solution)/shard_map/ppermute | solution.py:23
  23.5 4.8 %collective-permute-start.9 = (bf16[4,16,256]{2,1,0:T(8,128)(2,1)S(1)}, bf16[4,16,256]{2,1,0:T(8,128)(2,1)S(1)}, u32[]{:S(2)}, u32[]{:S(2)}) collective-permute-start(bf16[4,16,256]{2,1,0:T(8,128)(2,1)S(1)} %get-tuple-element.26), channel_id=1, source_target_pairs={{0,8},{1,9},{2,10},{3,11},{4,12},{5,13},{6,14},{7,15},{8,0},{9,1},... | collective-permute-start | bytes 98312 | tf_op jit(solution)/shard_map/ppermute | solution.py:23
  28.4 1.9 %collective-permute-start.11 = (bf16[4,16,256]{2,1,0:T(8,128)(2,1)S(1)}, bf16[4,16,256]{2,1,0:T(8,128)(2,1)S(1)}, u32[]{:S(2)}, u32[]{:S(2)}) collective-permute-start(bf16[4,16,256]{2,1,0:T(8,128)(2,1)S(1)} %get-tuple-element.28), channel_id=1, source_target_pairs={{0,1},{1,0},{2,3},{3,2},{4,5},{5,4},{6,7},{7,6},{8,9},{9,8},{10,11... | collective-permute-start | bytes 98312 | tf_op jit(solution)/shard_map/ppermute | solution.py:23
  28.4 4.0 %collective-permute-start.12 = (bf16[4,16,256]{2,1,0:T(8,128)(2,1)S(1)}, bf16[4,16,256]{2,1,0:T(8,128)(2,1)S(1)}, u32[]{:S(2)}, u32[]{:S(2)}) collective-permute-start(bf16[4,16,256]{2,1,0:T(8,128)(2,1)S(1)} %get-tuple-element.29), channel_id=1, source_target_pairs={{0,2},{1,3},{2,0},{3,1},{4,6},{5,7},{6,4},{7,5},{8,10},{9,11},{10,... | collective-permute-start | bytes 98312 | tf_op jit(solution)/shard_map/ppermute | solution.py:23
  29.9 3.3 %collective-permute-start.13 = (bf16[4,16,256]{2,1,0:T(8,128)(2,1)S(1)}, bf16[4,16,256]{2,1,0:T(8,128)(2,1)S(1)}, u32[]{:S(2)}, u32[]{:S(2)}) collective-permute-start(bf16[4,16,256]{2,1,0:T(8,128)(2,1)S(1)} %get-tuple-element.30), channel_id=1, source_target_pairs={{0,3},{1,2},{2,1},{3,0},{4,7},{5,6},{6,5},{7,4},{8,11},{9,10},{10,... | collective-permute-start | bytes 98312 | tf_op jit(solution)/shard_map/ppermute | solution.py:23
  37.8 1.3 %collective-permute-start.14 = (bf16[16,2048]{1,0:T(8,128)(2,1)S(1)}, bf16[16,2048]{1,0:T(8,128)(2,1)S(1)}, u32[]{:S(2)}, u32[]{:S(2)}) collective-permute-start(bf16[16,2048]{1,0:T(8,128)(2,1)S(1)} %get-tuple-element.32), channel_id=1, source_target_pairs={{0,1},{1,0},{2,3},{3,2},{4,5},{5,4},{6,7},{7,6},{8,9},{9,8},{10,11... | collective-permute-start | bytes 196616 | tf_op jit(solution)/shard_map/ppermute | solution.py:23
  39.1 4.3 %collective-permute-start.15 = (bf16[16,2048]{1,0:T(8,128)(2,1)S(1)}, bf16[16,2048]{1,0:T(8,128)(2,1)S(1)}, u32[]{:S(2)}, u32[]{:S(2)}) collective-permute-start(bf16[16,2048]{1,0:T(8,128)(2,1)S(1)} %fusion), channel_id=1, source_target_pairs={{0,2},{1,3},{2,0},{3,1},{4,6},{5,7},{6,4},{7,5},{8,10},{9,11},{10,... | collective-permute-start | bytes 196616 | tf_op jit(solution)/shard_map/ppermute | solution.py:23
  40.2 4.6 %collective-permute-start.16 = (bf16[16,2048]{1,0:T(8,128)(2,1)S(1)}, bf16[16,2048]{1,0:T(8,128)(2,1)S(1)}, u32[]{:S(2)}, u32[]{:S(2)}) collective-permute-start(bf16[16,2048]{1,0:T(8,128)(2,1)S(1)} %fusion), channel_id=1, source_target_pairs={{0,4},{1,5},{2,6},{3,7},{4,0},{5,1},{6,2},{7,3},{8,12},{9,13},{10,... | collective-permute-start | bytes 196616 | tf_op jit(solution)/shard_map/ppermute | solution.py:23
  40.9 5.2 %collective-permute-start.17 = (bf16[16,2048]{1,0:T(8,128)(2,1)S(1)}, bf16[16,2048]{1,0:T(8,128)(2,1)S(1)}, u32[]{:S(2)}, u32[]{:S(2)}) collective-permute-start(bf16[16,2048]{1,0:T(8,128)(2,1)S(1)} %fusion), channel_id=1, source_target_pairs={{0,6},{1,7},{2,4},{3,5},{4,2},{5,3},{6,0},{7,1},{8,14},{9,15},{10,... | collective-permute-start | bytes 196616 | tf_op jit(solution)/shard_map/ppermute | solution.py:23
  42.6 4.9 %collective-permute-start = (f32[8,4096]{1,0:T(8,128)S(1)}, f32[8,4096]{1,0:T(8,128)S(1)}, u32[]{:S(2)}, u32[]{:S(2)}) collective-permute-start(f32[8,4096]{1,0:T(8,128)S(1)} %get-tuple-element.20.targets), channel_id=1, source_target_pairs={{0,1},{1,0},{2,3},{3,2},{4,5},{5,4},{6,7},{7,6},{8,9},{9,8},{10,11... | collective-permute-start | bytes 393224 | tf_op jit(solution)/shard_map/ppermute | solution.py:23
  46.1 5.2 %collective-permute-start.18 = (bf16[16,2048]{1,0:T(8,128)(2,1)S(1)}, bf16[16,2048]{1,0:T(8,128)(2,1)S(1)}, u32[]{:S(2)}, u32[]{:S(2)}) collective-permute-start(bf16[16,2048]{1,0:T(8,128)(2,1)S(1)} %get-tuple-element.35), channel_id=1, source_target_pairs={{0,8},{1,9},{2,10},{3,11},{4,12},{5,13},{6,14},{7,15},{8,0},{9,1},... | collective-permute-start | bytes 196616 | tf_op jit(solution)/shard_map/ppermute | solution.py:23
  51.9 1.2 %collective-permute-start.19 = (f32[8,128]{1,0:T(8,128)S(1)}, f32[8,128]{1,0:T(8,128)S(1)}, u32[]{:S(2)}, u32[]{:S(2)}) collective-permute-start(f32[8,128]{1,0:T(8,128)S(1)} %get-tuple-element.34), channel_id=1, source_target_pairs={{0,1},{1,0},{2,3},{3,2},{4,5},{5,4},{6,7},{7,6},{8,9},{9,8},{10,11... | collective-permute-start | bytes 12296 | tf_op jit(solution)/shard_map/ppermute | solution.py:23
  (4 other events, 53.1 us)

commit v2 on v0

--- a/solution.py
+++ b/solution.py
@@ -184,7 +184,7 @@
     send[...] = total[:, pl.ds(partner, part)].astype(jnp.bfloat16)
 
 
-def partial_features(me, arrays, places, projection):
+def partial_features(me, arrays, places, projection, after):
     n = len(places)
     share = arrays[0].shape[1]
     depth, width = projection.shape
@@ -192,7 +192,7 @@
     return pl.pallas_call(
         functools.partial(features_kernel, places, len(arrays)),
         out_shape=[jax.ShapeDtypeStruct(half, jnp.float32), jax.ShapeDtypeStruct(half, jnp.bfloat16)],
-        in_specs=[SMEM] + [VMEM] * (len(arrays) + 1),
+        in_specs=[SMEM] + [VMEM] * (len(arrays) + 1) + [ANY],
         out_specs=[VMEM, VMEM],
         scratch_shapes=[
             pltpu.VMEM((LANES // 128, n * max(share, 8), 128), jnp.float32),
@@ -202,7 +202,7 @@
         compiler_params=pltpu.CompilerParams(vmem_limit_bytes=4 * MIB),
         cost_estimate=pl.CostEstimate(flops=600000000, bytes_accessed=34000000, transcendentals=0),
         name="features",
-    )(me, *arrays, in_vmem(projection))
+    )(me, *arrays, in_vmem(projection), after)
 
 
 def scores_kernel(me, targets, partner_targets, kept, *refs):
@@ -247,18 +247,23 @@
     whole = [(tokens, 0, tokens.shape[0]), (cotangent, 0, cotangent.shape[0])]
     whole += [(response_loss_mask.reshape(1, -1), 0, 1), (targets, 0, targets.shape[0])]
     tokens, cotangent, mask, targets = load("load_1", whole, (me,))
+    cut = far // 2
     column = [block] + [swap(block, NEAR * d, n) for d in range(1, far)]
-    (column,) = join("join_blocks", column, [[(d,) for d in range(far)]], block.shape, (mask,))
-    places = [[NEAR * d + k for d in range(far)] for k in range(NEAR)]
-    total = partial_lowrank("lowrank_1", me, tokens, [column], places[:1])
-    across = hold("hold", swap(column, 2, n), (total,))
-    total = partial_lowrank("lowrank_2", me, tokens, [swap(column, 1, n), across], places[1:3], (total,))
+    across = [swap(value, 2, n) for value in column]
+    places = [[[NEAR * d + k] for d in range(far)] for k in range(NEAR)]
+    blocks, owners = column + across[:cut], places[0] + places[2][:cut]
+    total = partial_lowrank("lowrank_1", me, tokens, blocks, owners)
+    picks = [[(i,) for i in range(2 * far)]]
+    (gathered,) = join("join_core", column + across, picks, block.shape, (total,))
+    other = swap(gathered, 1, n)
+    total = partial_lowrank("lowrank_2", me, tokens, across[cut:], places[2][cut:], (total,))
+    owners = [[k + 1 for part in places[0] + places[2] for k in part]]
 
     stages = [bits[i : i + 2] for i in range(2, len(bits), 2)] + [bits[:2]]
     left = span([b for stage in stages[1:] for b in stage])
     moves = span(stages[0])
-    owners = [[m ^ r for r in left] for m in moves]
-    rows = packed_grads(me, owners, tokens, [swap(across, 1, n)], places[3:], total, cotangent, mask)
+    targets_of = [[m ^ r for r in left] for m in moves]
+    rows = packed_grads(me, targets_of, tokens, [other], owners, total, cotangent, mask)
     rows = list(rows)
     rows[1] = hold("hold_rows", rows[1], (), HIDE)
     arrays = [rows[0]] + [swap(array, m, n) for array, m in zip(rows[1:], moves[1:])]
@@ -273,10 +278,10 @@
             kept.update({(src ^ m, r ^ m): (len(arrays), i) for i, (src, r) in enumerate(group)})
             arrays.append(swap(array, m, n))
         held = kept
+
+    places = [held[k, 0] for k in range(n)]
     partner_targets = swap(targets, 1, n)
-
-    places = [held[k, 0] for k in range(n)]
-    kept, send = partial_features(me, arrays, places, projection)
+    kept, send = partial_features(me, arrays, places, projection, partner_targets)
     kept = kept + swap(send, 1, n).astype(jnp.float32)
     for stage in [bits[1:3]] + [[bit] for bit in bits[3:]]:
         half = kept.astype(jnp.bfloat16)

time: 54.6 us -> 54.3 us (level)
  waiting for transfers between devices: 24.5 us -> 21.1 us
  starting transfers between devices: 19.3 us -> 22.3 us
    ppermute x19 -> x21, waiting for transfers between devices: 24.5 us -> 21.1 us  [swap(): return lax.ppermute(value, 'shard', [(s, s ^ bit) for s in range(n)])]
    ppermute x19 -> x21, starting transfers between devices: 19.3 us -> 22.3 us  [swap(): return lax.ppermute(value, 'shard', [(s, s ^ bit) for s in range(n)])]
  transfers between devices with their start and end apart: 19 -> 21, of which waited for: 14 -> 12; matrix products, arithmetic and copies ran while one was open for 0% -> 0% of each run, Pallas kernels for 7% -> 8%
where the time goes in v2:
time: 54.3 us; the launch traced here: 54.1 us
  starting transfers between devices  22.3 us (41%)
  waiting for transfers between devices  21.1 us (39%)
  Pallas kernels  9.68 us (18%)
  other arithmetic  0.74 us (1%)
    ppermute x21, starting transfers between devices, swap(): return lax.ppermute(value, 'shard', [(s, s ^ bit) for s in range(n)])  22.3 us
    ppermute x21, waiting for transfers between devices, swap(): return lax.ppermute(value, 'shard', [(s, s ^ bit) for s in range(n)])  21.1 us
    pallas_call x1, Pallas kernels, partial_features(): pl.pallas_call(functools.partial(features_kernel, places, len(arrays)), o...  4.5 us
    pallas_call x1, Pallas kernels, load(): pl.pallas_call(functools.partial(load_kernel, len(parts), [start for _, s...  2.39 us
    pallas_call x1, Pallas kernels, packed_grads(): pl.pallas_call(functools.partial(grads_kernel, owners, places), out_shape...  1.27 us
  transfers between devices with their start and end apart: 21, of which 12 were waited for; matrix products, arithmetic and copies ran while one was open for 0% of the time, Pallas kernels for 8%

profile of v2, /device:TPU:0, one launch (start us, length us, event | category | flops | bytes accessed | tf_op | source)
XLA Modules:
  0.0 54.1 jit_solution(1883723292394324640)
XLA Ops:
  0.0 3.0 %collective-permute-start.1 = (bf16[64,512]{1,0:T(8,128)(2,1)}, bf16[64,512]{1,0:T(8,128)(2,1)S(1)}, u32[]{:S(2)}, u32[]{:S(2)}) collective-permute-start(bf16[64,512]{1,0:T(8,128)(2,1)} %refs_0_.5), channel_id=1, source_target_pairs={{0,4},{1,5},{2,6},{3,7},{4,0},{5,1},{6,2},{7,3},{8,12},{9,13},{10,... | collective-permute-start | bytes 196616 | tf_op jit(solution)/shard_map/ppermute | solution.py:23
  3.0 2.6 %collective-permute-start.2 = (bf16[64,512]{1,0:T(8,128)(2,1)}, bf16[64,512]{1,0:T(8,128)(2,1)S(1)}, u32[]{:S(2)}, u32[]{:S(2)}) collective-permute-start(bf16[64,512]{1,0:T(8,128)(2,1)} %refs_0_.5), channel_id=1, source_target_pairs={{0,8},{1,9},{2,10},{3,11},{4,12},{5,13},{6,14},{7,15},{8,0},{9,1},... | collective-permute-start | bytes 196616 | tf_op jit(solution)/shard_map/ppermute | solution.py:23
  5.6 1.7 %collective-permute-start.4 = (bf16[64,512]{1,0:T(8,128)(2,1)}, bf16[64,512]{1,0:T(8,128)(2,1)S(1)}, u32[]{:S(2)}, u32[]{:S(2)}) collective-permute-start(bf16[64,512]{1,0:T(8,128)(2,1)} %refs_0_.5), channel_id=1, source_target_pairs={{0,2},{1,3},{2,0},{3,1},{4,6},{5,7},{6,4},{7,5},{8,10},{9,11},{10,... | collective-permute-start | bytes 196616 | tf_op jit(solution)/shard_map/ppermute | solution.py:23
  7.7 2.9 %collective-permute-done.2.refs_2_ = bf16[64,512]{1,0:T(8,128)(2,1)S(1)} collective-permute-done((bf16[64,512]{1,0:T(8,128)(2,1)}, bf16[64,512]{1,0:T(8,128)(2,1)S(1)}, u32[]{:S(2)}, u32[]{:S(2)}) %collective-permute-start.2) | collective-permute-done | bytes 65568 | tf_op jit(solution)/shard_map/ppermute | solution.py:23
  10.5 1.5 %collective-permute-start.6 = (bf16[64,512]{1,0:T(8,128)(2,1)S(1)}, bf16[64,512]{1,0:T(8,128)(2,1)S(1)}, u32[]{:S(2)}, u32[]{:S(2)}) collective-permute-start(bf16[64,512]{1,0:T(8,128)(2,1)S(1)} %collective-permute-done.2.refs_2_), channel_id=1, source_target_pairs={{0,2},{1,3},{2,0},{3,1},{4,6},{5,7},{6,4},{7,5},{8,10},{9,11},{10,... | collective-permute-start | bytes 196616 | tf_op jit(solution)/shard_map/ppermute | solution.py:23
  12.0 1.4 %collective-permute-start.7 = (bf16[64,512]{1,0:T(8,128)(2,1)S(1)}, bf16[64,512]{1,0:T(8,128)(2,1)S(1)}, u32[]{:S(2)}, u32[]{:S(2)}) collective-permute-start(bf16[64,512]{1,0:T(8,128)(2,1)S(1)} %collective-permute-done.3.refs_3_), channel_id=1, source_target_pairs={{0,2},{1,3},{2,0},{3,1},{4,6},{5,7},{6,4},{7,5},{8,10},{9,11},{10,... | collective-permute-start | bytes 196616 | tf_op jit(solution)/shard_map/ppermute | solution.py:23
  13.4 2.4 %load_1.1 = (bf16[256,8192]{1,0:T(8,128)(2,1)S(1)}, bf16[256,1024]{1,0:T(8,128)(2,1)S(1)}, s32[1,256]{1,0:T(1,128)S(1)}, f32[8,4096]{1,0:T(8,128)S(1)}) custom-call(bf16[256,8192]{1,0:T(8,128)(2,1)} %refs_0_.3, bf16[256,1024]{1,0:T(8,128)(2,1)} %refs_1_.1, s32[1,256]{1,0:T(1,128)} %bitcast.6, f32[8,4096]{1,0:T(8,128)} %refs_3_.1, s32[1]{0:T(128)} %bitcast.refs_4_.me), custom_call_target="tpu_custom_call" | custom-call | bytes 9701376 | tf_op jit(solution)/shard_map/load_1/pallas_call | solution.py:59
  17.4 1.1 %collective-permute-done.8.refs_0_ = bf16[8,64,512]{2,1,0:T(8,128)(2,1)S(1)} collective-permute-done((bf16[8,64,512]{2,1,0:T(8,128)(2,1)S(1)}, bf16[8,64,512]{2,1,0:T(8,128)(2,1)S(1)}, u32[]{:S(2)}, u32[]{:S(2)}) %collective-permute-start.8) | collective-permute-done | bytes 524320 | tf_op jit(solution)/shard_map/ppermute | solution.py:23
  18.5 1.3 %grads.1 = (bf16[4,16,256]{2,1,0:T(8,128)(2,1)S(1)}, bf16[4,16,256]{2,1,0:T(8,128)(2,1)S(1)}, bf16[4,16,256]{2,1,0:T(8,128)(2,1)S(1)}, bf16[4,16,256]{2,1,0:T(8,128)(2,1)S(1)}) custom-call(s32[1]{0:T(128)} %bitcast.refs_4_.me, bf16[256,8192]{1,0:T(8,128)(2,1)S(1)} %get-tuple-element.21.tokens, bf16[8,64,512]{2,1,0:T(8,128)(2,1)S(1)} %collective-permute-done.8.refs_0_, ...), custom_call_target="tpu_custom_call" | custom-call | flops 100000000 | bytes 2000000 | tf_op jit(solution)/shard_map/grads/pallas_call | solution.py:152
  20.2 3.3 %collective-permute-start.10 = (bf16[4,16,256]{2,1,0:T(8,128)(2,1)S(1)}, bf16[4,16,256]{2,1,0:T(8,128)(2,1)S(1)}, u32[]{:S(2)}, u32[]{:S(2)}) collective-permute-start(bf16[4,16,256]{2,1,0:T(8,128)(2,1)S(1)} %get-tuple-element.26), channel_id=1, source_target_pairs={{0,8},{1,9},{2,10},{3,11},{4,12},{5,13},{6,14},{7,15},{8,0},{9,1},... | collective-permute-start | bytes 98312 | tf_op jit(solution)/shard_map/ppermute | solution.py:23
  24.4 1.3 %collective-permute-done.10.refs_2_ = bf16[4,16,256]{2,1,0:T(8,128)(2,1)S(1)} collective-permute-done((bf16[4,16,256]{2,1,0:T(8,128)(2,1)S(1)}, bf16[4,16,256]{2,1,0:T(8,128)(2,1)S(1)}, u32[]{:S(2)}, u32[]{:S(2)}) %collective-permute-start.10) | collective-permute-done | bytes 32800 | tf_op jit(solution)/shard_map/ppermute | solution.py:23
  25.7 3.5 %collective-permute-done.11.refs_3_ = bf16[4,16,256]{2,1,0:T(8,128)(2,1)S(1)} collective-permute-done((bf16[4,16,256]{2,1,0:T(8,128)(2,1)S(1)}, bf16[4,16,256]{2,1,0:T(8,128)(2,1)S(1)}, u32[]{:S(2)}, u32[]{:S(2)}) %collective-permute-start.11) | collective-permute-done | bytes 32800 | tf_op jit(solution)/shard_map/ppermute | solution.py:23
  29.3 0.9 %collective-permute-start.13 = (bf16[4,16,256]{2,1,0:T(8,128)(2,1)S(1)}, bf16[4,16,256]{2,1,0:T(8,128)(2,1)S(1)}, u32[]{:S(2)}, u32[]{:S(2)}) collective-permute-start(bf16[4,16,256]{2,1,0:T(8,128)(2,1)S(1)} %get-tuple-element.29), channel_id=1, source_target_pairs={{0,2},{1,3},{2,0},{3,1},{4,6},{5,7},{6,4},{7,5},{8,10},{9,11},{10,... | collective-permute-start | bytes 98312 | tf_op jit(solution)/shard_map/ppermute | solution.py:23
  30.2 1.0 %collective-permute-start.14 = (bf16[4,16,256]{2,1,0:T(8,128)(2,1)S(1)}, bf16[4,16,256]{2,1,0:T(8,128)(2,1)S(1)}, u32[]{:S(2)}, u32[]{:S(2)}) collective-permute-start(bf16[4,16,256]{2,1,0:T(8,128)(2,1)S(1)} %get-tuple-element.30), channel_id=1, source_target_pairs={{0,3},{1,2},{2,1},{3,0},{4,7},{5,6},{6,5},{7,4},{8,11},{9,10},{10,... | collective-permute-start | bytes 98312 | tf_op jit(solution)/shard_map/ppermute | solution.py:23
  31.2 2.2 %collective-permute-done.13.refs_5_ = bf16[4,16,256]{2,1,0:T(8,128)(2,1)S(1)} collective-permute-done((bf16[4,16,256]{2,1,0:T(8,128)(2,1)S(1)}, bf16[4,16,256]{2,1,0:T(8,128)(2,1)S(1)}, u32[]{:S(2)}, u32[]{:S(2)}) %collective-permute-start.13) | collective-permute-done | bytes 32800 | tf_op jit(solution)/shard_map/ppermute | solution.py:23
  33.8 4.5 %features.1 = (f32[16,2048]{1,0:T(8,128)S(1)}, bf16[16,2048]{1,0:T(8,128)(2,1)S(1)}) custom-call(s32[1]{0:T(128)} %bitcast.refs_4_.me, bf16[4,16,256]{2,1,0:T(8,128)(2,1)S(1)} %get-tuple-element.24.refs_0_, bf16[4,16,256]{2,1,0:T(8,128)(2,1)S(1)} %collective-permute-done.9.refs_1_, bf16[4,16,256]{2,1,0:T(8,128)(2,1)S(1)} %collective-permute-done.10.refs_2_, ...), custom_call_target="tpu_custom_call" | custom-call | flops 600000000 | bytes 34000000 | tf_op jit(solution)/shard_map/features/pallas_call | solution.py:192
  38.4 1.1 %collective-permute-done.15 = bf16[16,2048]{1,0:T(8,128)(2,1)S(1)} collective-permute-done((bf16[16,2048]{1,0:T(8,128)(2,1)S(1)}, bf16[16,2048]{1,0:T(8,128)(2,1)S(1)}, u32[]{:S(2)}, u32[]{:S(2)}) %collective-permute-start.15) | collective-permute-done | bytes 65568 | tf_op jit(solution)/shard_map/ppermute | solution.py:23
  39.6 1.1 %collective-permute-start.16 = (bf16[16,2048]{1,0:T(8,128)(2,1)S(1)}, bf16[16,2048]{1,0:T(8,128)(2,1)S(1)}, u32[]{:S(2)}, u32[]{:S(2)}) collective-permute-start(bf16[16,2048]{1,0:T(8,128)(2,1)S(1)} %fusion), channel_id=1, source_target_pairs={{0,2},{1,3},{2,0},{3,1},{4,6},{5,7},{6,4},{7,5},{8,10},{9,11},{10,... | collective-permute-start | bytes 196616 | tf_op jit(solution)/shard_map/ppermute | solution.py:23
  40.7 2.5 %collective-permute-start.18 = (bf16[16,2048]{1,0:T(8,128)(2,1)S(1)}, bf16[16,2048]{1,0:T(8,128)(2,1)S(1)}, u32[]{:S(2)}, u32[]{:S(2)}) collective-permute-start(bf16[16,2048]{1,0:T(8,128)(2,1)S(1)} %fusion), channel_id=1, source_target_pairs={{0,6},{1,7},{2,4},{3,5},{4,2},{5,3},{6,0},{7,1},{8,14},{9,15},{10,... | collective-permute-start | bytes 196616 | tf_op jit(solution)/shard_map/ppermute | solution.py:23
  43.9 1.3 %collective-permute-done.17 = bf16[16,2048]{1,0:T(8,128)(2,1)S(1)} collective-permute-done((bf16[16,2048]{1,0:T(8,128)(2,1)S(1)}, bf16[16,2048]{1,0:T(8,128)(2,1)S(1)}, u32[]{:S(2)}, u32[]{:S(2)}) %collective-permute-start.17) | collective-permute-done | bytes 65568 | tf_op jit(solution)/shard_map/ppermute | solution.py:23
  45.2 1.2 %collective-permute-done.18 = bf16[16,2048]{1,0:T(8,128)(2,1)S(1)} collective-permute-done((bf16[16,2048]{1,0:T(8,128)(2,1)S(1)}, bf16[16,2048]{1,0:T(8,128)(2,1)S(1)}, u32[]{:S(2)}, u32[]{:S(2)}) %collective-permute-start.18) | collective-permute-done | bytes 65568 | tf_op jit(solution)/shard_map/ppermute | solution.py:23
  46.4 1.1 %collective-permute-start.19 = (bf16[16,2048]{1,0:T(8,128)(2,1)S(1)}, bf16[16,2048]{1,0:T(8,128)(2,1)S(1)}, u32[]{:S(2)}, u32[]{:S(2)}) collective-permute-start(bf16[16,2048]{1,0:T(8,128)(2,1)S(1)} %get-tuple-element.35), channel_id=1, source_target_pairs={{0,8},{1,9},{2,10},{3,11},{4,12},{5,13},{6,14},{7,15},{8,0},{9,1},... | collective-permute-start | bytes 196616 | tf_op jit(solution)/shard_map/ppermute | solution.py:23
  47.6 4.1 %collective-permute-done.19.refs_0_ = bf16[16,2048]{1,0:T(8,128)(2,1)S(1)} collective-permute-done((bf16[16,2048]{1,0:T(8,128)(2,1)S(1)}, bf16[16,2048]{1,0:T(8,128)(2,1)S(1)}, u32[]{:S(2)}, u32[]{:S(2)}) %collective-permute-start.19) | collective-permute-done | bytes 65568 | tf_op jit(solution)/shard_map/ppermute | solution.py:23
  52.3 1.2 %collective-permute-done.20 = f32[8,128]{1,0:T(8,128)S(1)} collective-permute-done((f32[8,128]{1,0:T(8,128)S(1)}, f32[8,128]{1,0:T(8,128)S(1)}, u32[]{:S(2)}, u32[]{:S(2)}) %collective-permute-start.20) | collective-permute-done | bytes 4128 | tf_op jit(solution)/shard_map/ppermute | solution.py:23
  (50 shorter events, 5.7 us)
Async XLA Ops:
  0.0 15.9 %copy-start = (bf16[64,512]{1,0:T(8,128)(2,1)S(1)}, bf16[64,512]{1,0:T(8,128)(2,1)}, u32[]{:S(2)}) copy-start(bf16[64,512]{1,0:T(8,128)(2,1)} %refs_0_.5) | copy-start | bytes 196612
  0.0 7.4 %collective-permute-start.1 = (bf16[64,512]{1,0:T(8,128)(2,1)}, bf16[64,512]{1,0:T(8,128)(2,1)S(1)}, u32[]{:S(2)}, u32[]{:S(2)}) collective-permute-start(bf16[64,512]{1,0:T(8,128)(2,1)} %refs_0_.5), channel_id=1, source_target_pairs={{0,4},{1,5},{2,6},{3,7},{4,0},{5,1},{6,2},{7,3},{8,12},{9,13},{10,... | collective-permute-start | bytes 196616 | tf_op jit(solution)/shard_map/ppermute | solution.py:23
  3.0 7.5 %collective-permute-start.2 = (bf16[64,512]{1,0:T(8,128)(2,1)}, bf16[64,512]{1,0:T(8,128)(2,1)S(1)}, u32[]{:S(2)}, u32[]{:S(2)}) collective-permute-start(bf16[64,512]{1,0:T(8,128)(2,1)} %refs_0_.5), channel_id=1, source_target_pairs={{0,8},{1,9},{2,10},{3,11},{4,12},{5,13},{6,14},{7,15},{8,0},{9,1},... | collective-permute-start | bytes 196616 | tf_op jit(solution)/shard_map/ppermute | solution.py:23
  5.6 6.4 %collective-permute-start.3 = (bf16[64,512]{1,0:T(8,128)(2,1)}, bf16[64,512]{1,0:T(8,128)(2,1)S(1)}, u32[]{:S(2)}, u32[]{:S(2)}) collective-permute-start(bf16[64,512]{1,0:T(8,128)(2,1)} %refs_0_.5), channel_id=1, source_target_pairs={{0,12},{1,13},{2,14},{3,15},{4,8},{5,9},{6,10},{7,11},{8,4},{9,5},... | collective-permute-start | bytes 196616 | tf_op jit(solution)/shard_map/ppermute | solution.py:23
  5.6 10.2 %collective-permute-start.4 = (bf16[64,512]{1,0:T(8,128)(2,1)}, bf16[64,512]{1,0:T(8,128)(2,1)S(1)}, u32[]{:S(2)}, u32[]{:S(2)}) collective-permute-start(bf16[64,512]{1,0:T(8,128)(2,1)} %refs_0_.5), channel_id=1, source_target_pairs={{0,2},{1,3},{2,0},{3,1},{4,6},{5,7},{6,4},{7,5},{8,10},{9,11},{10,... | collective-permute-start | bytes 196616 | tf_op jit(solution)/shard_map/ppermute | solution.py:23
  7.4 8.5 %collective-permute-start.5 = (bf16[64,512]{1,0:T(8,128)(2,1)S(1)}, bf16[64,512]{1,0:T(8,128)(2,1)S(1)}, u32[]{:S(2)}, u32[]{:S(2)}) collective-permute-start(bf16[64,512]{1,0:T(8,128)(2,1)S(1)} %collective-permute-done.1.refs_1_), channel_id=1, source_target_pairs={{0,2},{1,3},{2,0},{3,1},{4,6},{5,7},{6,4},{7,5},{8,10},{9,11},{10,... | collective-permute-start | bytes 196616 | tf_op jit(solution)/shard_map/ppermute | solution.py:23
  10.5 6.0 %collective-permute-start.6 = (bf16[64,512]{1,0:T(8,128)(2,1)S(1)}, bf16[64,512]{1,0:T(8,128)(2,1)S(1)}, u32[]{:S(2)}, u32[]{:S(2)}) collective-permute-start(bf16[64,512]{1,0:T(8,128)(2,1)S(1)} %collective-permute-done.2.refs_2_), channel_id=1, source_target_pairs={{0,2},{1,3},{2,0},{3,1},{4,6},{5,7},{6,4},{7,5},{8,10},{9,11},{10,... | collective-permute-start | bytes 196616 | tf_op jit(solution)/shard_map/ppermute | solution.py:23
  12.0 4.4 %collective-permute-start.7 = (bf16[64,512]{1,0:T(8,128)(2,1)S(1)}, bf16[64,512]{1,0:T(8,128)(2,1)S(1)}, u32[]{:S(2)}, u32[]{:S(2)}) collective-permute-start(bf16[64,512]{1,0:T(8,128)(2,1)S(1)} %collective-permute-done.3.refs_3_), channel_id=1, source_target_pairs={{0,2},{1,3},{2,0},{3,1},{4,6},{5,7},{6,4},{7,5},{8,10},{9,11},{10,... | collective-permute-start | bytes 196616 | tf_op jit(solution)/shard_map/ppermute | solution.py:23
  16.5 2.0 %collective-permute-start.8 = (bf16[8,64,512]{2,1,0:T(8,128)(2,1)S(1)}, bf16[8,64,512]{2,1,0:T(8,128)(2,1)S(1)}, u32[]{:S(2)}, u32[]{:S(2)}) collective-permute-start(bf16[8,64,512]{2,1,0:T(8,128)(2,1)S(1)} %join_core.1), channel_id=1, source_target_pairs={{0,1},{1,0},{2,3},{3,2},{4,5},{5,4},{6,7},{7,6},{8,9},{9,8},{10,11... | collective-permute-start | bytes 1572872 | tf_op jit(solution)/shard_map/ppermute | solution.py:23
  16.6 14.5 %collective-permute-start = (f32[8,4096]{1,0:T(8,128)S(1)}, f32[8,4096]{1,0:T(8,128)S(1)}, u32[]{:S(2)}, u32[]{:S(2)}) collective-permute-start(f32[8,4096]{1,0:T(8,128)S(1)} %get-tuple-element.20.targets), channel_id=1, source_target_pairs={{0,1},{1,0},{2,3},{3,2},{4,5},{5,4},{6,7},{7,6},{8,9},{9,8},{10,11... | collective-permute-start | bytes 393224 | tf_op jit(solution)/shard_map/ppermute | solution.py:23
  19.8 13.9 %slice-start = ((s8[33554432]{0:T(1024)(128)(4,1)}), s8[4194304]{0:T(1024)(128)(4,1)S(1)}, s32[]{:S(2)}) async-start(s8[33554432]{0:T(1024)(128)(4,1)} %bitcast.4), calls=%async_computation | async-start | bytes 8388608
  19.8 13.9 %slice-start.1 = ((s8[33554432]{0:T(1024)(128)(4,1)}), s8[4194304]{0:T(1024)(128)(4,1)S(1)}, s32[]{:S(2)}) async-start(s8[33554432]{0:T(1024)(128)(4,1)} %bitcast.4), calls=%async_computation.1 | async-start | bytes 8388608
  19.9 4.5 %collective-permute-start.9 = (bf16[4,16,256]{2,1,0:T(8,128)(2,1)S(1)}, bf16[4,16,256]{2,1,0:T(8,128)(2,1)S(1)}, u32[]{:S(2)}, u32[]{:S(2)}) collective-permute-start(bf16[4,16,256]{2,1,0:T(8,128)(2,1)S(1)} %hold_rows.1), channel_id=1, source_target_pairs={{0,4},{1,5},{2,6},{3,7},{4,0},{5,1},{6,2},{7,3},{8,12},{9,13},{10,... | collective-permute-start | bytes 98312 | tf_op jit(solution)/shard_map/ppermute | solution.py:23
  20.2 5.5 %collective-permute-start.10 = (bf16[4,16,256]{2,1,0:T(8,128)(2,1)S(1)}, bf16[4,16,256]{2,1,0:T(8,128)(2,1)S(1)}, u32[]{:S(2)}, u32[]{:S(2)}) collective-permute-start(bf16[4,16,256]{2,1,0:T(8,128)(2,1)S(1)} %get-tuple-element.26), channel_id=1, source_target_pairs={{0,8},{1,9},{2,10},{3,11},{4,12},{5,13},{6,14},{7,15},{8,0},{9,1},... | collective-permute-start | bytes 98312 | tf_op jit(solution)/shard_map/ppermute | solution.py:23
  23.5 5.7 %collective-permute-start.11 = (bf16[4,16,256]{2,1,0:T(8,128)(2,1)S(1)}, bf16[4,16,256]{2,1,0:T(8,128)(2,1)S(1)}, u32[]{:S(2)}, u32[]{:S(2)}) collective-permute-start(bf16[4,16,256]{2,1,0:T(8,128)(2,1)S(1)} %get-tuple-element.27), channel_id=1, source_target_pairs={{0,12},{1,13},{2,14},{3,15},{4,8},{5,9},{6,10},{7,11},{8,4},{9,5},... | collective-permute-start | bytes 98312 | tf_op jit(solution)/shard_map/ppermute | solution.py:23
  29.2 1.9 %collective-permute-start.12 = (bf16[4,16,256]{2,1,0:T(8,128)(2,1)S(1)}, bf16[4,16,256]{2,1,0:T(8,128)(2,1)S(1)}, u32[]{:S(2)}, u32[]{:S(2)}) collective-permute-start(bf16[4,16,256]{2,1,0:T(8,128)(2,1)S(1)} %get-tuple-element.28), channel_id=1, source_target_pairs={{0,1},{1,0},{2,3},{3,2},{4,5},{5,4},{6,7},{7,6},{8,9},{9,8},{10,11... | collective-permute-start | bytes 98312 | tf_op jit(solution)/shard_map/ppermute | solution.py:23
  29.3 4.1 %collective-permute-start.13 = (bf16[4,16,256]{2,1,0:T(8,128)(2,1)S(1)}, bf16[4,16,256]{2,1,0:T(8,128)(2,1)S(1)}, u32[]{:S(2)}, u32[]{:S(2)}) collective-permute-start(bf16[4,16,256]{2,1,0:T(8,128)(2,1)S(1)} %get-tuple-element.29), channel_id=1, source_target_pairs={{0,2},{1,3},{2,0},{3,1},{4,6},{5,7},{6,4},{7,5},{8,10},{9,11},{10,... | collective-permute-start | bytes 98312 | tf_op jit(solution)/shard_map/ppermute | solution.py:23
  30.2 3.5 %collective-permute-start.14 = (bf16[4,16,256]{2,1,0:T(8,128)(2,1)S(1)}, bf16[4,16,256]{2,1,0:T(8,128)(2,1)S(1)}, u32[]{:S(2)}, u32[]{:S(2)}) collective-permute-start(bf16[4,16,256]{2,1,0:T(8,128)(2,1)S(1)} %get-tuple-element.30), channel_id=1, source_target_pairs={{0,3},{1,2},{2,1},{3,0},{4,7},{5,6},{6,5},{7,4},{8,11},{9,10},{10,... | collective-permute-start | bytes 98312 | tf_op jit(solution)/shard_map/ppermute | solution.py:23
  38.3 1.3 %collective-permute-start.15 = (bf16[16,2048]{1,0:T(8,128)(2,1)S(1)}, bf16[16,2048]{1,0:T(8,128)(2,1)S(1)}, u32[]{:S(2)}, u32[]{:S(2)}) collective-permute-start(bf16[16,2048]{1,0:T(8,128)(2,1)S(1)} %get-tuple-element.32), channel_id=1, source_target_pairs={{0,1},{1,0},{2,3},{3,2},{4,5},{5,4},{6,7},{7,6},{8,9},{9,8},{10,11... | collective-permute-start | bytes 196616 | tf_op jit(solution)/shard_map/ppermute | solution.py:23
  39.6 4.3 %collective-permute-start.16 = (bf16[16,2048]{1,0:T(8,128)(2,1)S(1)}, bf16[16,2048]{1,0:T(8,128)(2,1)S(1)}, u32[]{:S(2)}, u32[]{:S(2)}) collective-permute-start(bf16[16,2048]{1,0:T(8,128)(2,1)S(1)} %fusion), channel_id=1, source_target_pairs={{0,2},{1,3},{2,0},{3,1},{4,6},{5,7},{6,4},{7,5},{8,10},{9,11},{10,... | collective-permute-start | bytes 196616 | tf_op jit(solution)/shard_map/ppermute | solution.py:23
  40.7 4.6 %collective-permute-start.17 = (bf16[16,2048]{1,0:T(8,128)(2,1)S(1)}, bf16[16,2048]{1,0:T(8,128)(2,1)S(1)}, u32[]{:S(2)}, u32[]{:S(2)}) collective-permute-start(bf16[16,2048]{1,0:T(8,128)(2,1)S(1)} %fusion), channel_id=1, source_target_pairs={{0,4},{1,5},{2,6},{3,7},{4,0},{5,1},{6,2},{7,3},{8,12},{9,13},{10,... | collective-permute-start | bytes 196616 | tf_op jit(solution)/shard_map/ppermute | solution.py:23
  40.7 5.7 %collective-permute-start.18 = (bf16[16,2048]{1,0:T(8,128)(2,1)S(1)}, bf16[16,2048]{1,0:T(8,128)(2,1)S(1)}, u32[]{:S(2)}, u32[]{:S(2)}) collective-permute-start(bf16[16,2048]{1,0:T(8,128)(2,1)S(1)} %fusion), channel_id=1, source_target_pairs={{0,6},{1,7},{2,4},{3,5},{4,2},{5,3},{6,0},{7,1},{8,14},{9,15},{10,... | collective-permute-start | bytes 196616 | tf_op jit(solution)/shard_map/ppermute | solution.py:23
  46.4 5.2 %collective-permute-start.19 = (bf16[16,2048]{1,0:T(8,128)(2,1)S(1)}, bf16[16,2048]{1,0:T(8,128)(2,1)S(1)}, u32[]{:S(2)}, u32[]{:S(2)}) collective-permute-start(bf16[16,2048]{1,0:T(8,128)(2,1)S(1)} %get-tuple-element.35), channel_id=1, source_target_pairs={{0,8},{1,9},{2,10},{3,11},{4,12},{5,13},{6,14},{7,15},{8,0},{9,1},... | collective-permute-start | bytes 196616 | tf_op jit(solution)/shard_map/ppermute | solution.py:23
  52.2 1.2 %collective-permute-start.20 = (f32[8,128]{1,0:T(8,128)S(1)}, f32[8,128]{1,0:T(8,128)S(1)}, u32[]{:S(2)}, u32[]{:S(2)}) collective-permute-start(f32[8,128]{1,0:T(8,128)S(1)} %get-tuple-element.34), channel_id=1, source_target_pairs={{0,1},{1,0},{2,3},{3,2},{4,5},{5,4},{6,7},{7,6},{8,9},{9,8},{10,11... | collective-permute-start | bytes 12296 | tf_op jit(solution)/shard_map/ppermute | solution.py:23
  (6 other events, 83.5 us)

commit v3 on v2

--- a/solution.py
+++ b/solution.py
@@ -265,29 +265,30 @@
     targets_of = [[m ^ r for r in left] for m in moves]
     rows = packed_grads(me, targets_of, tokens, [other], owners, total, cotangent, mask)
     rows = list(rows)
-    rows[1] = hold("hold_rows", rows[1], (), HIDE)
-    arrays = [rows[0]] + [swap(array, m, n) for array, m in zip(rows[1:], moves[1:])]
-    held = {(m, r): (a, i) for a, m in enumerate(moves) for i, r in enumerate(left)}
+    rows[-1] = hold("hold_rows", rows[-1], (), HIDE)
+    arrays = [swap(array, m, n) for array, m in zip(rows[:0:-1], moves[:0:-1])] + [rows[0]]
+    held = {(m, r): (a, i) for a, m in enumerate(moves[::-1]) for i, r in enumerate(left)}
     for number, stage in enumerate(stages[1:]):
         moves, left = span(stage), span([b for later in stages[number + 2 :] for b in later])
         pairs = [[(src, r ^ m) for src in sorted({s for s, _ in held}) for r in left] for m in moves]
         picks = [[held[pair] for pair in group] for group in pairs[1:]]
         sent = join(f"join_rows_{number}", arrays, picks, rows[0].shape[1:])
-        kept = {pair: held[pair] for pair in pairs[0]}
-        for m, group, array in zip(moves[1:], pairs[1:], sent):
-            kept.update({(src ^ m, r ^ m): (len(arrays), i) for i, (src, r) in enumerate(group)})
-            arrays.append(swap(array, m, n))
-        held = kept
+        came = [swap(array, m, n) for array, m in zip(sent[::-1], moves[:0:-1])]
+        kept = {pair: (held[pair][0] + len(came), held[pair][1]) for pair in pairs[0]}
+        for a, (m, group) in enumerate(zip(moves[:0:-1], pairs[:0:-1])):
+            kept.update({(src ^ m, r ^ m): (a, i) for i, (src, r) in enumerate(group)})
+        arrays, held = came + arrays, kept
+    partner_targets = swap(targets, 1, n)
 
     places = [held[k, 0] for k in range(n)]
-    partner_targets = swap(targets, 1, n)
     kept, send = partial_features(me, arrays, places, projection, partner_targets)
     kept = kept + swap(send, 1, n).astype(jnp.float32)
     for stage in [bits[1:3]] + [[bit] for bit in bits[3:]]:
         half = kept.astype(jnp.bfloat16)
-        arrived = [swap(half, m, n) for m in span(stage)[1:]]
+        arrived = [swap(half, m, n) for m in span(stage)[:0:-1]]
         if bits[-1] not in stage:
-            kept = kept + sum(value.astype(jnp.float32) for value in arrived)
+            for value in arrived:
+                kept = kept + value.astype(jnp.float32)
     mine, send = partial_scores(me, targets, partner_targets, kept, arrived)
     total = mine + swap(send, 1, n)
     scale = lax.rsqrt(total[:, n : 2 * n] / PDIM + 1e-06)

time: 54.3 us -> 53 us (0.976)
  waiting for transfers between devices: 21.1 us -> 19 us
  starting transfers between devices: 22.3 us -> 23.2 us
    ppermute x21, waiting for transfers between devices: 21.1 us -> 19 us  [swap(): return lax.ppermute(value, 'shard', [(s, s ^ bit) for s in range(n)])]
    ppermute x21, starting transfers between devices: 22.3 us -> 23.2 us  [swap(): return lax.ppermute(value, 'shard', [(s, s ^ bit) for s in range(n)])]
  transfers between devices with their start and end apart: 21 -> 21, of which waited for: 12 -> 11; matrix products, arithmetic and copies ran while one was open for 0% -> 0% of each run, Pallas kernels for 8% -> 9%
where the time goes in v3:
time: 53 us; the launch traced here: 52.9 us
  starting transfers between devices  23.2 us (44%)
  waiting for transfers between devices  19 us (36%)
  Pallas kernels  9.68 us (18%)
  other arithmetic  0.74 us (1%)
    ppermute x21, starting transfers between devices, swap(): return lax.ppermute(value, 'shard', [(s, s ^ bit) for s in range(n)])  23.2 us
    ppermute x21, waiting for transfers between devices, swap(): return lax.ppermute(value, 'shard', [(s, s ^ bit) for s in range(n)])  19 us
    pallas_call x1, Pallas kernels, partial_features(): pl.pallas_call(functools.partial(features_kernel, places, len(arrays)), o...  4.5 us
    pallas_call x1, Pallas kernels, load(): pl.pallas_call(functools.partial(load_kernel, len(parts), [start for _, s...  2.39 us
    pallas_call x1, Pallas kernels, packed_grads(): pl.pallas_call(functools.partial(grads_kernel, owners, places), out_shape...  1.27 us
  transfers between devices with their start and end apart: 21, of which 11 were waited for; matrix products, arithmetic and copies ran while one was open for 0% of the time, Pallas kernels for 9%

profile of v3, /device:TPU:0, one launch (start us, length us, event | category | flops | bytes accessed | tf_op | source)
XLA Modules:
  0.0 52.9 jit_solution(11647226833620133373)
XLA Ops:
  0.0 3.0 %collective-permute-start.1 = (bf16[64,512]{1,0:T(8,128)(2,1)}, bf16[64,512]{1,0:T(8,128)(2,1)S(1)}, u32[]{:S(2)}, u32[]{:S(2)}) collective-permute-start(bf16[64,512]{1,0:T(8,128)(2,1)} %refs_0_.5), channel_id=1, source_target_pairs={{0,4},{1,5},{2,6},{3,7},{4,0},{5,1},{6,2},{7,3},{8,12},{9,13},{10,... | collective-permute-start | bytes 196616 | tf_op jit(solution)/shard_map/ppermute | solution.py:23
  3.0 2.6 %collective-permute-start.2 = (bf16[64,512]{1,0:T(8,128)(2,1)}, bf16[64,512]{1,0:T(8,128)(2,1)S(1)}, u32[]{:S(2)}, u32[]{:S(2)}) collective-permute-start(bf16[64,512]{1,0:T(8,128)(2,1)} %refs_0_.5), channel_id=1, source_target_pairs={{0,8},{1,9},{2,10},{3,11},{4,12},{5,13},{6,14},{7,15},{8,0},{9,1},... | collective-permute-start | bytes 196616 | tf_op jit(solution)/shard_map/ppermute | solution.py:23
  5.6 1.7 %collective-permute-start.4 = (bf16[64,512]{1,0:T(8,128)(2,1)}, bf16[64,512]{1,0:T(8,128)(2,1)S(1)}, u32[]{:S(2)}, u32[]{:S(2)}) collective-permute-start(bf16[64,512]{1,0:T(8,128)(2,1)} %refs_0_.5), channel_id=1, source_target_pairs={{0,2},{1,3},{2,0},{3,1},{4,6},{5,7},{6,4},{7,5},{8,10},{9,11},{10,... | collective-permute-start | bytes 196616 | tf_op jit(solution)/shard_map/ppermute | solution.py:23
  7.7 2.9 %collective-permute-done.2.refs_2_ = bf16[64,512]{1,0:T(8,128)(2,1)S(1)} collective-permute-done((bf16[64,512]{1,0:T(8,128)(2,1)}, bf16[64,512]{1,0:T(8,128)(2,1)S(1)}, u32[]{:S(2)}, u32[]{:S(2)}) %collective-permute-start.2) | collective-permute-done | bytes 65568 | tf_op jit(solution)/shard_map/ppermute | solution.py:23
  10.5 1.5 %collective-permute-start.6 = (bf16[64,512]{1,0:T(8,128)(2,1)S(1)}, bf16[64,512]{1,0:T(8,128)(2,1)S(1)}, u32[]{:S(2)}, u32[]{:S(2)}) collective-permute-start(bf16[64,512]{1,0:T(8,128)(2,1)S(1)} %collective-permute-done.2.refs_2_), channel_id=1, source_target_pairs={{0,2},{1,3},{2,0},{3,1},{4,6},{5,7},{6,4},{7,5},{8,10},{9,11},{10,... | collective-permute-start | bytes 196616 | tf_op jit(solution)/shard_map/ppermute | solution.py:23
  12.0 1.4 %collective-permute-start.7 = (bf16[64,512]{1,0:T(8,128)(2,1)S(1)}, bf16[64,512]{1,0:T(8,128)(2,1)S(1)}, u32[]{:S(2)}, u32[]{:S(2)}) collective-permute-start(bf16[64,512]{1,0:T(8,128)(2,1)S(1)} %collective-permute-done.3.refs_3_), channel_id=1, source_target_pairs={{0,2},{1,3},{2,0},{3,1},{4,6},{5,7},{6,4},{7,5},{8,10},{9,11},{10,... | collective-permute-start | bytes 196616 | tf_op jit(solution)/shard_map/ppermute | solution.py:23
  13.4 2.4 %load_1.1 = (bf16[256,8192]{1,0:T(8,128)(2,1)S(1)}, bf16[256,1024]{1,0:T(8,128)(2,1)S(1)}, s32[1,256]{1,0:T(1,128)S(1)}, f32[8,4096]{1,0:T(8,128)S(1)}) custom-call(bf16[256,8192]{1,0:T(8,128)(2,1)} %refs_0_.3, bf16[256,1024]{1,0:T(8,128)(2,1)} %refs_1_.1, s32[1,256]{1,0:T(1,128)} %bitcast.6, f32[8,4096]{1,0:T(8,128)} %refs_3_.1, s32[1]{0:T(128)} %bitcast.refs_4_.me), custom_call_target="tpu_custom_call" | custom-call | bytes 9701376 | tf_op jit(solution)/shard_map/load_1/pallas_call | solution.py:59
  17.4 1.1 %collective-permute-done.8.refs_0_ = bf16[8,64,512]{2,1,0:T(8,128)(2,1)S(1)} collective-permute-done((bf16[8,64,512]{2,1,0:T(8,128)(2,1)S(1)}, bf16[8,64,512]{2,1,0:T(8,128)(2,1)S(1)}, u32[]{:S(2)}, u32[]{:S(2)}) %collective-permute-start.8) | collective-permute-done | bytes 524320 | tf_op jit(solution)/shard_map/ppermute | solution.py:23
  18.5 1.3 %grads.1 = (bf16[4,16,256]{2,1,0:T(8,128)(2,1)S(1)}, bf16[4,16,256]{2,1,0:T(8,128)(2,1)S(1)}, bf16[4,16,256]{2,1,0:T(8,128)(2,1)S(1)}, bf16[4,16,256]{2,1,0:T(8,128)(2,1)S(1)}) custom-call(s32[1]{0:T(128)} %bitcast.refs_4_.me, bf16[256,8192]{1,0:T(8,128)(2,1)S(1)} %get-tuple-element.21.tokens, bf16[8,64,512]{2,1,0:T(8,128)(2,1)S(1)} %collective-permute-done.8.refs_0_, ...), custom_call_target="tpu_custom_call" | custom-call | flops 100000000 | bytes 2000000 | tf_op jit(solution)/shard_map/grads/pallas_call | solution.py:152
  19.9 3.0 %collective-permute-start.9 = (bf16[4,16,256]{2,1,0:T(8,128)(2,1)S(1)}, bf16[4,16,256]{2,1,0:T(8,128)(2,1)S(1)}, u32[]{:S(2)}, u32[]{:S(2)}) collective-permute-start(bf16[4,16,256]{2,1,0:T(8,128)(2,1)S(1)} %hold_rows.1), channel_id=1, source_target_pairs={{0,12},{1,13},{2,14},{3,15},{4,8},{5,9},{6,10},{7,11},{8,4},{9,5},... | collective-permute-start | bytes 98312 | tf_op jit(solution)/shard_map/ppermute | solution.py:23
  22.9 1.4 %collective-permute-start.11 = (bf16[4,16,256]{2,1,0:T(8,128)(2,1)S(1)}, bf16[4,16,256]{2,1,0:T(8,128)(2,1)S(1)}, u32[]{:S(2)}, u32[]{:S(2)}) collective-permute-start(bf16[4,16,256]{2,1,0:T(8,128)(2,1)S(1)} %get-tuple-element.26), channel_id=1, source_target_pairs={{0,4},{1,5},{2,6},{3,7},{4,0},{5,1},{6,2},{7,3},{8,12},{9,13},{10,... | collective-permute-start | bytes 98312 | tf_op jit(solution)/shard_map/ppermute | solution.py:23
  24.4 1.4 %collective-permute-done.9.refs_0_.refs_3_ = bf16[4,16,256]{2,1,0:T(8,128)(2,1)S(1)} collective-permute-done((bf16[4,16,256]{2,1,0:T(8,128)(2,1)S(1)}, bf16[4,16,256]{2,1,0:T(8,128)(2,1)S(1)}, u32[]{:S(2)}, u32[]{:S(2)}) %collective-permute-start.9) | collective-permute-done | bytes 32800 | tf_op jit(solution)/shard_map/ppermute | solution.py:23
  25.7 2.0 %collective-permute-done.10.refs_1_.refs_4_ = bf16[4,16,256]{2,1,0:T(8,128)(2,1)S(1)} collective-permute-done((bf16[4,16,256]{2,1,0:T(8,128)(2,1)S(1)}, bf16[4,16,256]{2,1,0:T(8,128)(2,1)S(1)}, u32[]{:S(2)}, u32[]{:S(2)}) %collective-permute-start.10) | collective-permute-done | bytes 32800 | tf_op jit(solution)/shard_map/ppermute | solution.py:23
  28.7 1.0 %collective-permute-start.14 = (bf16[4,16,256]{2,1,0:T(8,128)(2,1)S(1)}, bf16[4,16,256]{2,1,0:T(8,128)(2,1)S(1)}, u32[]{:S(2)}, u32[]{:S(2)}) collective-permute-start(bf16[4,16,256]{2,1,0:T(8,128)(2,1)S(1)} %get-tuple-element.30), channel_id=1, source_target_pairs={{0,1},{1,0},{2,3},{3,2},{4,5},{5,4},{6,7},{7,6},{8,9},{9,8},{10,11... | collective-permute-start | bytes 98312 | tf_op jit(solution)/shard_map/ppermute | solution.py:23
  29.7 1.5 %collective-permute-done.12.refs_0_ = bf16[4,16,256]{2,1,0:T(8,128)(2,1)S(1)} collective-permute-done((bf16[4,16,256]{2,1,0:T(8,128)(2,1)S(1)}, bf16[4,16,256]{2,1,0:T(8,128)(2,1)S(1)}, u32[]{:S(2)}, u32[]{:S(2)}) %collective-permute-start.12) | collective-permute-done | bytes 32800 | tf_op jit(solution)/shard_map/ppermute | solution.py:23
  32.1 4.5 %features.1 = (f32[16,2048]{1,0:T(8,128)S(1)}, bf16[16,2048]{1,0:T(8,128)(2,1)S(1)}) custom-call(s32[1]{0:T(128)} %bitcast.refs_4_.me, bf16[4,16,256]{2,1,0:T(8,128)(2,1)S(1)} %collective-permute-done.12.refs_0_, bf16[4,16,256]{2,1,0:T(8,128)(2,1)S(1)} %collective-permute-done.13.refs_1_, bf16[4,16,256]{2,1,0:T(8,128)(2,1)S(1)} %collective-permute-done.14.refs_2_, ...), custom_call_target="tpu_custom_call" | custom-call | flops 600000000 | bytes 34000000 | tf_op jit(solution)/shard_map/features/pallas_call | solution.py:192
  36.7 1.2 %collective-permute-done.15 = bf16[16,2048]{1,0:T(8,128)(2,1)S(1)} collective-permute-done((bf16[16,2048]{1,0:T(8,128)(2,1)S(1)}, bf16[16,2048]{1,0:T(8,128)(2,1)S(1)}, u32[]{:S(2)}, u32[]{:S(2)}) %collective-permute-start.15) | collective-permute-done | bytes 65568 | tf_op jit(solution)/shard_map/ppermute | solution.py:23
  37.9 1.2 %collective-permute-start.16 = (bf16[16,2048]{1,0:T(8,128)(2,1)S(1)}, bf16[16,2048]{1,0:T(8,128)(2,1)S(1)}, u32[]{:S(2)}, u32[]{:S(2)}) collective-permute-start(bf16[16,2048]{1,0:T(8,128)(2,1)S(1)} %fusion), channel_id=1, source_target_pairs={{0,6},{1,7},{2,4},{3,5},{4,2},{5,3},{6,0},{7,1},{8,14},{9,15},{10,... | collective-permute-start | bytes 196616 | tf_op jit(solution)/shard_map/ppermute | solution.py:23
  39.2 1.0 %collective-permute-start.17 = (bf16[16,2048]{1,0:T(8,128)(2,1)S(1)}, bf16[16,2048]{1,0:T(8,128)(2,1)S(1)}, u32[]{:S(2)}, u32[]{:S(2)}) collective-permute-start(bf16[16,2048]{1,0:T(8,128)(2,1)S(1)} %fusion), channel_id=1, source_target_pairs={{0,4},{1,5},{2,6},{3,7},{4,0},{5,1},{6,2},{7,3},{8,12},{9,13},{10,... | collective-permute-start | bytes 196616 | tf_op jit(solution)/shard_map/ppermute | solution.py:23
  40.1 1.4 %collective-permute-start.18 = (bf16[16,2048]{1,0:T(8,128)(2,1)S(1)}, bf16[16,2048]{1,0:T(8,128)(2,1)S(1)}, u32[]{:S(2)}, u32[]{:S(2)}) collective-permute-start(bf16[16,2048]{1,0:T(8,128)(2,1)S(1)} %fusion), channel_id=1, source_target_pairs={{0,2},{1,3},{2,0},{3,1},{4,6},{5,7},{6,4},{7,5},{8,10},{9,11},{10,... | collective-permute-start | bytes 196616 | tf_op jit(solution)/shard_map/ppermute | solution.py:23
  41.5 2.3 %collective-permute-done.16 = bf16[16,2048]{1,0:T(8,128)(2,1)S(1)} collective-permute-done((bf16[16,2048]{1,0:T(8,128)(2,1)S(1)}, bf16[16,2048]{1,0:T(8,128)(2,1)S(1)}, u32[]{:S(2)}, u32[]{:S(2)}) %collective-permute-start.16) | collective-permute-done | bytes 65568 | tf_op jit(solution)/shard_map/ppermute | solution.py:23
  44.5 2.1 %collective-permute-start.19 = (bf16[16,2048]{1,0:T(8,128)(2,1)S(1)}, bf16[16,2048]{1,0:T(8,128)(2,1)S(1)}, u32[]{:S(2)}, u32[]{:S(2)}) collective-permute-start(bf16[16,2048]{1,0:T(8,128)(2,1)S(1)} %get-tuple-element.35), channel_id=1, source_target_pairs={{0,8},{1,9},{2,10},{3,11},{4,12},{5,13},{6,14},{7,15},{8,0},{9,1},... | collective-permute-start | bytes 196616 | tf_op jit(solution)/shard_map/ppermute | solution.py:23
  46.6 3.8 %collective-permute-done.19.refs_0_ = bf16[16,2048]{1,0:T(8,128)(2,1)S(1)} collective-permute-done((bf16[16,2048]{1,0:T(8,128)(2,1)S(1)}, bf16[16,2048]{1,0:T(8,128)(2,1)S(1)}, u32[]{:S(2)}, u32[]{:S(2)}) %collective-permute-start.19) | collective-permute-done | bytes 65568 | tf_op jit(solution)/shard_map/ppermute | solution.py:23
  51.0 1.2 %collective-permute-done.20 = f32[8,128]{1,0:T(8,128)S(1)} collective-permute-done((f32[8,128]{1,0:T(8,128)S(1)}, f32[8,128]{1,0:T(8,128)S(1)}, u32[]{:S(2)}, u32[]{:S(2)}) %collective-permute-start.20) | collective-permute-done | bytes 4128 | tf_op jit(solution)/shard_map/ppermute | solution.py:23
  (50 shorter events, 5.7 us)
Async XLA Ops:
  0.0 15.9 %copy-start = (bf16[64,512]{1,0:T(8,128)(2,1)S(1)}, bf16[64,512]{1,0:T(8,128)(2,1)}, u32[]{:S(2)}) copy-start(bf16[64,512]{1,0:T(8,128)(2,1)} %refs_0_.5) | copy-start | bytes 196612
  0.0 7.4 %collective-permute-start.1 = (bf16[64,512]{1,0:T(8,128)(2,1)}, bf16[64,512]{1,0:T(8,128)(2,1)S(1)}, u32[]{:S(2)}, u32[]{:S(2)}) collective-permute-start(bf16[64,512]{1,0:T(8,128)(2,1)} %refs_0_.5), channel_id=1, source_target_pairs={{0,4},{1,5},{2,6},{3,7},{4,0},{5,1},{6,2},{7,3},{8,12},{9,13},{10,... | collective-permute-start | bytes 196616 | tf_op jit(solution)/shard_map/ppermute | solution.py:23
  3.0 7.5 %collective-permute-start.2 = (bf16[64,512]{1,0:T(8,128)(2,1)}, bf16[64,512]{1,0:T(8,128)(2,1)S(1)}, u32[]{:S(2)}, u32[]{:S(2)}) collective-permute-start(bf16[64,512]{1,0:T(8,128)(2,1)} %refs_0_.5), channel_id=1, source_target_pairs={{0,8},{1,9},{2,10},{3,11},{4,12},{5,13},{6,14},{7,15},{8,0},{9,1},... | collective-permute-start | bytes 196616 | tf_op jit(solution)/shard_map/ppermute | solution.py:23
  5.6 6.4 %collective-permute-start.3 = (bf16[64,512]{1,0:T(8,128)(2,1)}, bf16[64,512]{1,0:T(8,128)(2,1)S(1)}, u32[]{:S(2)}, u32[]{:S(2)}) collective-permute-start(bf16[64,512]{1,0:T(8,128)(2,1)} %refs_0_.5), channel_id=1, source_target_pairs={{0,12},{1,13},{2,14},{3,15},{4,8},{5,9},{6,10},{7,11},{8,4},{9,5},... | collective-permute-start | bytes 196616 | tf_op jit(solution)/shard_map/ppermute | solution.py:23
  5.6 10.2 %collective-permute-start.4 = (bf16[64,512]{1,0:T(8,128)(2,1)}, bf16[64,512]{1,0:T(8,128)(2,1)S(1)}, u32[]{:S(2)}, u32[]{:S(2)}) collective-permute-start(bf16[64,512]{1,0:T(8,128)(2,1)} %refs_0_.5), channel_id=1, source_target_pairs={{0,2},{1,3},{2,0},{3,1},{4,6},{5,7},{6,4},{7,5},{8,10},{9,11},{10,... | collective-permute-start | bytes 196616 | tf_op jit(solution)/shard_map/ppermute | solution.py:23
  7.4 8.5 %collective-permute-start.5 = (bf16[64,512]{1,0:T(8,128)(2,1)S(1)}, bf16[64,512]{1,0:T(8,128)(2,1)S(1)}, u32[]{:S(2)}, u32[]{:S(2)}) collective-permute-start(bf16[64,512]{1,0:T(8,128)(2,1)S(1)} %collective-permute-done.1.refs_1_), channel_id=1, source_target_pairs={{0,2},{1,3},{2,0},{3,1},{4,6},{5,7},{6,4},{7,5},{8,10},{9,11},{10,... | collective-permute-start | bytes 196616 | tf_op jit(solution)/shard_map/ppermute | solution.py:23
  10.5 6.0 %collective-permute-start.6 = (bf16[64,512]{1,0:T(8,128)(2,1)S(1)}, bf16[64,512]{1,0:T(8,128)(2,1)S(1)}, u32[]{:S(2)}, u32[]{:S(2)}) collective-permute-start(bf16[64,512]{1,0:T(8,128)(2,1)S(1)} %collective-permute-done.2.refs_2_), channel_id=1, source_target_pairs={{0,2},{1,3},{2,0},{3,1},{4,6},{5,7},{6,4},{7,5},{8,10},{9,11},{10,... | collective-permute-start | bytes 196616 | tf_op jit(solution)/shard_map/ppermute | solution.py:23
  12.0 4.4 %collective-permute-start.7 = (bf16[64,512]{1,0:T(8,128)(2,1)S(1)}, bf16[64,512]{1,0:T(8,128)(2,1)S(1)}, u32[]{:S(2)}, u32[]{:S(2)}) collective-permute-start(bf16[64,512]{1,0:T(8,128)(2,1)S(1)} %collective-permute-done.3.refs_3_), channel_id=1, source_target_pairs={{0,2},{1,3},{2,0},{3,1},{4,6},{5,7},{6,4},{7,5},{8,10},{9,11},{10,... | collective-permute-start | bytes 196616 | tf_op jit(solution)/shard_map/ppermute | solution.py:23
  16.5 2.0 %collective-permute-start.8 = (bf16[8,64,512]{2,1,0:T(8,128)(2,1)S(1)}, bf16[8,64,512]{2,1,0:T(8,128)(2,1)S(1)}, u32[]{:S(2)}, u32[]{:S(2)}) collective-permute-start(bf16[8,64,512]{2,1,0:T(8,128)(2,1)S(1)} %join_core.1), channel_id=1, source_target_pairs={{0,1},{1,0},{2,3},{3,2},{4,5},{5,4},{6,7},{7,6},{8,9},{9,8},{10,11... | collective-permute-start | bytes 1572872 | tf_op jit(solution)/shard_map/ppermute | solution.py:23
  16.6 13.1 %collective-permute-start = (f32[8,4096]{1,0:T(8,128)S(1)}, f32[8,4096]{1,0:T(8,128)S(1)}, u32[]{:S(2)}, u32[]{:S(2)}) collective-permute-start(f32[8,4096]{1,0:T(8,128)S(1)} %get-tuple-element.20.targets), channel_id=1, source_target_pairs={{0,1},{1,0},{2,3},{3,2},{4,5},{5,4},{6,7},{7,6},{8,9},{9,8},{10,11... | collective-permute-start | bytes 393224 | tf_op jit(solution)/shard_map/ppermute | solution.py:23
  19.8 12.3 %slice-start = ((s8[33554432]{0:T(1024)(128)(4,1)}), s8[4194304]{0:T(1024)(128)(4,1)S(1)}, s32[]{:S(2)}) async-start(s8[33554432]{0:T(1024)(128)(4,1)} %bitcast.4), calls=%async_computation | async-start | bytes 8388608
  19.8 12.3 %slice-start.1 = ((s8[33554432]{0:T(1024)(128)(4,1)}), s8[4194304]{0:T(1024)(128)(4,1)S(1)}, s32[]{:S(2)}) async-start(s8[33554432]{0:T(1024)(128)(4,1)} %bitcast.4), calls=%async_computation.1 | async-start | bytes 8388608
  19.9 5.8 %collective-permute-start.9 = (bf16[4,16,256]{2,1,0:T(8,128)(2,1)S(1)}, bf16[4,16,256]{2,1,0:T(8,128)(2,1)S(1)}, u32[]{:S(2)}, u32[]{:S(2)}) collective-permute-start(bf16[4,16,256]{2,1,0:T(8,128)(2,1)S(1)} %hold_rows.1), channel_id=1, source_target_pairs={{0,12},{1,13},{2,14},{3,15},{4,8},{5,9},{6,10},{7,11},{8,4},{9,5},... | collective-permute-start | bytes 98312 | tf_op jit(solution)/shard_map/ppermute | solution.py:23
  22.9 4.8 %collective-permute-start.10 = (bf16[4,16,256]{2,1,0:T(8,128)(2,1)S(1)}, bf16[4,16,256]{2,1,0:T(8,128)(2,1)S(1)}, u32[]{:S(2)}, u32[]{:S(2)}) collective-permute-start(bf16[4,16,256]{2,1,0:T(8,128)(2,1)S(1)} %get-tuple-element.25), channel_id=1, source_target_pairs={{0,8},{1,9},{2,10},{3,11},{4,12},{5,13},{6,14},{7,15},{8,0},{9,1},... | collective-permute-start | bytes 98312 | tf_op jit(solution)/shard_map/ppermute | solution.py:23
  22.9 4.8 %collective-permute-start.11 = (bf16[4,16,256]{2,1,0:T(8,128)(2,1)S(1)}, bf16[4,16,256]{2,1,0:T(8,128)(2,1)S(1)}, u32[]{:S(2)}, u32[]{:S(2)}) collective-permute-start(bf16[4,16,256]{2,1,0:T(8,128)(2,1)S(1)} %get-tuple-element.26), channel_id=1, source_target_pairs={{0,4},{1,5},{2,6},{3,7},{4,0},{5,1},{6,2},{7,3},{8,12},{9,13},{10,... | collective-permute-start | bytes 98312 | tf_op jit(solution)/shard_map/ppermute | solution.py:23
  27.8 3.4 %collective-permute-start.12 = (bf16[4,16,256]{2,1,0:T(8,128)(2,1)S(1)}, bf16[4,16,256]{2,1,0:T(8,128)(2,1)S(1)}, u32[]{:S(2)}, u32[]{:S(2)}) collective-permute-start(bf16[4,16,256]{2,1,0:T(8,128)(2,1)S(1)} %get-tuple-element.28), channel_id=1, source_target_pairs={{0,3},{1,2},{2,1},{3,0},{4,7},{5,6},{6,5},{7,4},{8,11},{9,10},{10,... | collective-permute-start | bytes 98312 | tf_op jit(solution)/shard_map/ppermute | solution.py:23
  27.8 4.2 %collective-permute-start.13 = (bf16[4,16,256]{2,1,0:T(8,128)(2,1)S(1)}, bf16[4,16,256]{2,1,0:T(8,128)(2,1)S(1)}, u32[]{:S(2)}, u32[]{:S(2)}) collective-permute-start(bf16[4,16,256]{2,1,0:T(8,128)(2,1)S(1)} %get-tuple-element.29), channel_id=1, source_target_pairs={{0,2},{1,3},{2,0},{3,1},{4,6},{5,7},{6,4},{7,5},{8,10},{9,11},{10,... | collective-permute-start | bytes 98312 | tf_op jit(solution)/shard_map/ppermute | solution.py:23
  28.7 3.3 %collective-permute-start.14 = (bf16[4,16,256]{2,1,0:T(8,128)(2,1)S(1)}, bf16[4,16,256]{2,1,0:T(8,128)(2,1)S(1)}, u32[]{:S(2)}, u32[]{:S(2)}) collective-permute-start(bf16[4,16,256]{2,1,0:T(8,128)(2,1)S(1)} %get-tuple-element.30), channel_id=1, source_target_pairs={{0,1},{1,0},{2,3},{3,2},{4,5},{5,4},{6,7},{7,6},{8,9},{9,8},{10,11... | collective-permute-start | bytes 98312 | tf_op jit(solution)/shard_map/ppermute | solution.py:23
  36.6 1.3 %collective-permute-start.15 = (bf16[16,2048]{1,0:T(8,128)(2,1)S(1)}, bf16[16,2048]{1,0:T(8,128)(2,1)S(1)}, u32[]{:S(2)}, u32[]{:S(2)}) collective-permute-start(bf16[16,2048]{1,0:T(8,128)(2,1)S(1)} %get-tuple-element.32), channel_id=1, source_target_pairs={{0,1},{1,0},{2,3},{3,2},{4,5},{5,4},{6,7},{7,6},{8,9},{9,8},{10,11... | collective-permute-start | bytes 196616 | tf_op jit(solution)/shard_map/ppermute | solution.py:23
  37.9 5.8 %collective-permute-start.16 = (bf16[16,2048]{1,0:T(8,128)(2,1)S(1)}, bf16[16,2048]{1,0:T(8,128)(2,1)S(1)}, u32[]{:S(2)}, u32[]{:S(2)}) collective-permute-start(bf16[16,2048]{1,0:T(8,128)(2,1)S(1)} %fusion), channel_id=1, source_target_pairs={{0,6},{1,7},{2,4},{3,5},{4,2},{5,3},{6,0},{7,1},{8,14},{9,15},{10,... | collective-permute-start | bytes 196616 | tf_op jit(solution)/shard_map/ppermute | solution.py:23
  39.2 4.6 %collective-permute-start.17 = (bf16[16,2048]{1,0:T(8,128)(2,1)S(1)}, bf16[16,2048]{1,0:T(8,128)(2,1)S(1)}, u32[]{:S(2)}, u32[]{:S(2)}) collective-permute-start(bf16[16,2048]{1,0:T(8,128)(2,1)S(1)} %fusion), channel_id=1, source_target_pairs={{0,4},{1,5},{2,6},{3,7},{4,0},{5,1},{6,2},{7,3},{8,12},{9,13},{10,... | collective-permute-start | bytes 196616 | tf_op jit(solution)/shard_map/ppermute | solution.py:23
  40.1 4.3 %collective-permute-start.18 = (bf16[16,2048]{1,0:T(8,128)(2,1)S(1)}, bf16[16,2048]{1,0:T(8,128)(2,1)S(1)}, u32[]{:S(2)}, u32[]{:S(2)}) collective-permute-start(bf16[16,2048]{1,0:T(8,128)(2,1)S(1)} %fusion), channel_id=1, source_target_pairs={{0,2},{1,3},{2,0},{3,1},{4,6},{5,7},{6,4},{7,5},{8,10},{9,11},{10,... | collective-permute-start | bytes 196616 | tf_op jit(solution)/shard_map/ppermute | solution.py:23
  44.5 5.9 %collective-permute-start.19 = (bf16[16,2048]{1,0:T(8,128)(2,1)S(1)}, bf16[16,2048]{1,0:T(8,128)(2,1)S(1)}, u32[]{:S(2)}, u32[]{:S(2)}) collective-permute-start(bf16[16,2048]{1,0:T(8,128)(2,1)S(1)} %get-tuple-element.35), channel_id=1, source_target_pairs={{0,8},{1,9},{2,10},{3,11},{4,12},{5,13},{6,14},{7,15},{8,0},{9,1},... | collective-permute-start | bytes 196616 | tf_op jit(solution)/shard_map/ppermute | solution.py:23
  51.0 1.2 %collective-permute-start.20 = (f32[8,128]{1,0:T(8,128)S(1)}, f32[8,128]{1,0:T(8,128)S(1)}, u32[]{:S(2)}, u32[]{:S(2)}) collective-permute-start(f32[8,128]{1,0:T(8,128)S(1)} %get-tuple-element.34), channel_id=1, source_target_pairs={{0,1},{1,0},{2,3},{3,2},{4,5},{5,4},{6,7},{7,6},{8,9},{9,8},{10,11... | collective-permute-start | bytes 12296 | tf_op jit(solution)/shard_map/ppermute | solution.py:23
  (6 other events, 73.5 us)
